TPU v7x, 512 devices: a whole 4x4x16 slice. The times are simulated.
512 devices in a mesh: wide: 32 (over y, z_lo), blk: 16 (over x, z_hi, core).
Axes of the slice: x: 4, y: 4, z: 16 (z_hi: 2, z_lo: 8; z = z_hi * 8 + z_lo), core: 2. Of those that a mesh axis runs over, the one named last changes fastest.
Arguments:
- source_strength: bfloat16 [16, 128, 128, 256], P('blk', 'wide'), may hold values from -0.75 to 0.75
- adjoint_strength: bfloat16 [16, 128, 128, 256], P('blk', 'wide'), may hold values from -0.75 to 0.75
- node_points: bfloat16 [16, 128, 3, 128], P('blk', 'wide'), may hold values from -2 to 2
- near_rows: int32 [16, 128, 32], P('blk', 'wide'), may hold values from 0 to 127, as said below
- counts_rows: int32 [16, 128], P('blk', 'wide'), may hold values from 1 to 32
- near_cols: int32 [16, 128, 16], P('blk', 'wide'), may hold values from 0 to 63, as said below
- counts_cols: int32 [16, 128], P('blk', 'wide'), may hold values from 1 to 16
Outputs:
- shape_gradient: float32 [16, 128, 3, 128], P('blk', 'wide')
Inputs may be any that keep to these rules, and one draw needn't show every extreme that they name: `near_rows`: for each block, its first counts_rows entries are distinct and ascending; the entries after them are unused. `near_cols`: for each block, its first counts_cols entries are distinct and ascending; the entries after them are unused.
All inputs are finite; a program needn't handle non-finite values.
Results may differ from a plain program's by a relative error of at most 0.0003.
Values may be sent and summed in bfloat16 or wider, within the bound.
A program may use at most 64 MiB of HBM per device.

v0:
```python
import jax
import jax.numpy as jnp
from jax import lax
from jax.sharding import PartitionSpec as P

EPS2 = 0.04


def pair_sum(
    own_points, own_values, far_points, far_values, partner_lists, counts, lowest, extent, per_turn
):
    blocks, listed = partner_lists.shape
    all_slots = blocks * listed
    partner = partner_lists.reshape(all_slots)
    owners = lax.broadcasted_iota(jnp.int32, (blocks, listed), 0).reshape(all_slots)
    active = (lax.broadcasted_iota(jnp.int32, (blocks, listed), 1) < counts[:, None]).reshape(
        all_slots
    )
    active = active & (partner >= lowest) & (partner < lowest + extent)
    ranking = jnp.argsort(
        jnp.where(active, 0, all_slots).astype(jnp.int32) + jnp.arange(all_slots, dtype=jnp.int32)
    )
    live_count = jnp.sum(active.astype(jnp.int32))
    own_index = jnp.pad(owners[ranking], (0, per_turn))
    far_index = jnp.pad(jnp.clip(partner[ranking] - lowest, 0, extent - 1), (0, per_turn))
    size_block = own_points.shape[-1]

    def step(step_index, running):
        offset = step_index * per_turn
        own_batch = lax.dynamic_slice_in_dim(own_index, offset, per_turn)
        far_batch = lax.dynamic_slice_in_dim(far_index, offset, per_turn)
        valid = (offset + jnp.arange(per_turn, dtype=jnp.int32) < live_count).astype(jnp.float32)
        weights = jnp.einsum(
            "gik,gjk->gij",
            own_values[own_batch],
            far_values[far_batch],
            preferred_element_type=jnp.float32,
        )
        own_batch_points = own_points[own_batch].astype(jnp.float32)
        far_batch_points = far_points[far_batch].astype(jnp.float32)
        separation = far_batch_points[:, :, None, :] - own_batch_points[:, :, :, None]
        distance = jnp.sum(separation * separation, axis=1) + EPS2
        inverse = lax.rsqrt(distance)
        scaled = weights * (inverse * inverse * inverse) * valid[:, None, None]
        contrib = jnp.sum(separation * scaled[:, None, :, :], axis=3)
        return running.at[own_batch].add(contrib)

    turns = (live_count + per_turn - 1) // per_turn
    return lax.fori_loop(0, turns, step, jnp.zeros((blocks, 3, size_block), jnp.float32))


def shards(
    source_strength, adjoint_strength, node_points, near_rows, counts_rows, near_cols, counts_cols
):
    per_device = source_strength.shape[1]
    size_block = source_strength.shape[2]
    conditions = source_strength.shape[3]
    own_points = node_points[0]
    own_source = source_strength[0]
    own_adjoint = adjoint_strength[0]
    row_lists = near_rows[0]
    row_counts = counts_rows[0]
    column_lists = near_cols[0]
    column_counts = counts_cols[0]
    panel_source, panel_points = (
        lax.all_gather(source_strength, "wide", axis=1, tiled=True),
        lax.all_gather(node_points, "wide", axis=1, tiled=True),
    )
    term_rows = pair_sum(
        own_points,
        own_adjoint,
        panel_points[0],
        panel_source[0],
        row_lists,
        row_counts,
        0,
        panel_source.shape[1],
        16,
    )
    column_adjoint, column_points = (
        lax.all_gather(adjoint_strength, "blk", axis=0, tiled=True),
        lax.all_gather(node_points, "blk", axis=0, tiled=True),
    )
    col_blocks = column_adjoint.shape[0] * per_device
    term_columns = pair_sum(
        own_points,
        own_source,
        column_points.reshape(col_blocks, 3, size_block),
        column_adjoint.reshape(col_blocks, size_block, conditions),
        column_lists,
        column_counts,
        0,
        col_blocks,
        16,
    )
    return (term_rows + term_columns)[None]


def solution(mesh):
    return jax.shard_map(
        shards,
        mesh=mesh,
        in_specs=(
            P("blk", "wide", None, None),
            P("blk", "wide", None, None),
            P("blk", "wide", None, None),
            P("blk", "wide", None),
            P("blk", "wide"),
            P("blk", "wide", None),
            P("blk", "wide"),
        ),
        out_specs=P("blk", "wide", None, None),
        check_vma=False,
    )
```

profile of v0, /device:TPU:4, one launch (start us, length us, event | category | flops | bytes accessed | tf_op | source)
XLA Modules:
  0.0 502.3 jit_solution(7287572324150749818)
XLA Ops:
  6.5 0.7 all-gather.5.cloned.1.call-update
  7.3 0.7 all-gather.3.cloned.1.call-update
  8.0 1.4 convert_reduce_fusion.1
  10.0 0.8 reshape_squeeze.6
  12.1 1.4 convert_reduce_fusion
  14.2 0.8 reshape_squeeze.7
  14.9 0.7 iota_compare_fusion.1
  15.8 2.5 sort.34
  18.3 1.2 gather_fusion.9
  19.7 1.2 gather_fusion.8
  20.9 0.7 iota_compare_fusion
  21.8 2.0 sort.35
  23.8 0.8 gather_fusion.11
  24.7 0.8 gather_fusion.10
  25.4 48.2 %all_gather.14 = bf16[16,4,3,128]{3,1,2,0:T(4,128)(2,1)S(1)} all-gather(bf16[1,4,3,128]{3,1,2,0:T(4,128)(2,1)} %param.13), channel_id=1, replica_groups=mesh['wide'=32,'blk'=16] {'blk'}, dimensions={0}, use_global_device_ids=true | all-gather | bytes 52224 | tf_op jit(solution)/shard_map/all_gather | solution.py:82
  73.8 131.3 %all_gather.12 = bf16[1,128,3,128]{3,2,0,1:T(4,128)(2,1)S(1)} all-gather(bf16[1,4,3,128]{3,2,0,1:T(4,128)(2,1)S(1)} %copy.30), channel_id=1, replica_groups=mesh['wide'=32,'blk'=16] {'wide'}, dimensions={1}, use_global_device_ids=true | all-gather | bytes 101376 | tf_op jit(solution)/shard_map/all_gather | solution.py:67
  205.1 12.2 %while.21 = (s32[]{:T(128)}, f32[4,3,128]{2,1,0:T(4,128)S(1)}, s32[]{:T(128)}, s32[80]{0:T(128)S(1)}, s32[80]{0:T(128)S(1)}, /*index=5*/bf16[64,3,128]{2,1,0:T(4...) while((s32[]{:T(128)}, f32[4,3,128]{2,1,0:T(4,128)S(1)}, ...), condition=%wide.region_13.14_spmd, body=%wide.region_9.13_spmd.sunk | while | flops 139999376 | bytes 10814463 | solution.py:49
  206.5 2.1 fusion.30
  209.2 2.8 gather_fusion.5
  212.7 1.7 fusion.31
  214.3 1.9 fusion.32
  216.2 1.1 scatter_fusion.1
  217.3 171.0 %all-gather.3.cloned.1.call-done = bf16[1,128,128,256]{3,2,0,1:T(8,128)(2,1)} async-done(((bf16[1,4,128,256]{3,2,0,1:T(8,128)(2,1)}), bf16[1,128,128,256]{3,2,0,1:T(8,128)(2,1)}) %all-gather.3.cloned.1.call-update) | async-done | bytes 8388624 | tf_op jit(solution)/shard_map/all_gather | solution.py:66
  388.3 106.5 %while.20 = (s32[]{:T(128)}, f32[4,3,128]{2,1,0:T(4,128)S(1)}, s32[]{:T(128)}, s32[144]{0:T(256)S(1)}, s32[144]{0:T(256)S(1)}, /*index=5*/bf16[128,3,128]{2,1,0:...) while((s32[]{:T(128)}, f32[4,3,128]{2,1,0:T(4,128)S(1)}, ...), condition=%wide.region_6.7_spmd, body=%wide.region_2.6_spmd.sunk | while | flops 139999376 | bytes 10814463 | solution.py:49
  389.6 2.1 fusion.25
  392.4 4.0 gather_fusion.1
  396.9 1.7 fusion.26
  398.6 1.9 fusion.27
  400.5 1.1 scatter_fusion
  403.0 2.1 fusion.25
  405.7 4.0 gather_fusion.1
  410.3 1.7 fusion.26
  411.9 1.9 fusion.27
  413.8 1.1 scatter_fusion
  416.3 2.1 fusion.25
  419.0 4.0 gather_fusion.1
  423.6 1.7 fusion.26
  425.3 1.9 fusion.27
  427.1 1.1 scatter_fusion
  429.6 2.1 fusion.25
  432.3 4.0 gather_fusion.1
  436.9 1.7 fusion.26
  438.6 1.9 fusion.27
  440.4 1.1 scatter_fusion
  442.9 2.1 fusion.25
  445.6 4.0 gather_fusion.1
  450.2 1.7 fusion.26
  451.9 1.9 fusion.27
  453.7 1.1 scatter_fusion
  456.2 2.1 fusion.25
  458.9 4.0 gather_fusion.1
  463.5 1.7 fusion.26
  465.2 1.9 fusion.27
  467.1 1.1 scatter_fusion
  469.5 2.1 fusion.25
  472.3 4.0 gather_fusion.1
  476.8 1.7 fusion.26
  478.5 1.9 fusion.27
  480.4 1.1 scatter_fusion
  482.8 2.1 fusion.25
  485.6 4.0 gather_fusion.1
  490.2 1.7 fusion.26
  491.8 1.9 fusion.27
  493.7 1.1 scatter_fusion
  (115 shorter events, 24.8 us)
Async XLA Ops:
  6.5 198.6 %copy-start = (bf16[1,4,128,256]{3,2,1,0:T(8,128)(2,1)S(1)}, bf16[1,4,128,256]{3,2,1,0:T(8,128)(2,1)}, u32[]{:S(2)}) copy-start(bf16[1,4,128,256]{3,2,1,0:T(8,128)(2,1)} %param.11) | copy-start | bytes 786436
  6.5 198.6 %all-gather.5.cloned.1.call-start = ((), (), s32[]{:S(2)}) async-start(), calls=%async_computation.1 | async-start | bytes 4456448 | tf_op jit(solution)/shard_map/all_gather | solution.py:81
  7.3 381.1 %all-gather.3.cloned.1.call-start = ((), (), s32[]{:S(2)}) async-start(), calls=%async_computation | async-start | bytes 8650752 | tf_op jit(solution)/shard_map/all_gather | solution.py:66
  205.1 183.2 %copy-start.1 = (bf16[1,4,128,256]{3,2,1,0:T(8,128)(2,1)S(1)}, bf16[1,4,128,256]{3,2,1,0:T(8,128)(2,1)}, u32[]{:S(2)}) copy-start(bf16[1,4,128,256]{3,2,1,0:T(8,128)(2,1)} %param.12) | copy-start | bytes 786436
Sparse Core Ops, SparseCore 0:
  10.6 125.5 all-gather.4
  138.3 249.9 all-gather.2
where the time goes:
time: 504 us; the launch traced here: 502 us
  blocking collectives  180 us (36%)
  waiting for transfers between devices  172 us (34%)
  other arithmetic  61.4 us (12%)
  local copies, waits for them, and re-layouts  58.2 us (12%)
  matrix products  15 us (3%)
  between operations  14.8 us (3%)
    all_gather x1, waiting for transfers between devices, shards(): lax.all_gather(source_strength, 'wide', axis=1, tiled=True)  171 us
    all_gather x1, blocking collectives, shards(): lax.all_gather(node_points, 'wide', axis=1, tiled=True)  131 us
    all_gather x1, blocking collectives, shards(): lax.all_gather(node_points, 'blk', axis=0, tiled=True)  48.2 us
    gather x9, local copies, waits for them, and re-layouts, step(): far_values[far_batch]  34.8 us
    reduce_sum x9, other arithmetic, step(): distance = jnp.sum(separation * separation, axis=1) + EPS2  18.9 us
    reduce_sum x9, other arithmetic, step(): contrib = jnp.sum(separation * scaled[:, None, :, :], axis=3)  16.7 us
    dot_general x9, matrix products, step(): jnp.einsum('gik,gjk->gij', own_values[own_batch], far_values[far_batch],...  15 us
    scatter-add x9, other arithmetic, step(): return running.at[own_batch].add(contrib)  10.2 us
  transfers between devices with their start and end apart: 2, of which 1 were waited for; matrix products, arithmetic and copies ran while one was open for 6% of the time, Pallas kernels for 0%

commit v1 on v0

v1 whole, which is shorter than its diff:
```python
import functools

import jax
import jax.numpy as jnp
from jax import lax
from jax.experimental import pallas as pl
from jax.experimental.pallas import tpu as pltpu
from jax.sharding import PartitionSpec as P

EPS2 = 0.04
MESH = pl.DeviceIdType.MESH
F32 = jnp.float32

NZ = 8
HALF = NZ // 2
AHEAD = NZ
SIBLING = AHEAD + HALF
SOURCES_Y = SIBLING + 2
MAX_PAIRS_ROWS = 6


class Place:
    def __init__(self, nx, ny):
        self.nx, self.ny = nx, ny
        self.wide, self.blk = lax.axis_index("wide"), lax.axis_index("blk")
        self.y, self.z = self.wide // NZ, self.wide % NZ
        self.x, self.h, self.c = self.blk // 4, (self.blk // 2) % 2, self.blk % 2

    def at(self, y=None, z=None, x=None, h=None, c=None):
        pick = lambda given, mine: mine if given is None else given
        wide = pick(y, self.y) * NZ + pick(z, self.z)
        blk = pick(x, self.x) * 4 + pick(h, self.h) * 2 + pick(c, self.c)
        return {"wide": wide, "blk": blk}

    def beside(self, right):
        if right:
            crosses = (self.z == NZ - 1).astype(jnp.int32)
            z = (self.z + 1) % NZ
        else:
            crosses = (self.z == 0).astype(jnp.int32)
            z = (self.z + NZ - 1) % NZ
        return self.at(z=z, h=(self.h + crosses) % 2)

    def others_z(self):
        return [((self.z + d) % NZ, self.at(z=(self.z + d) % NZ)) for d in range(1, NZ)]

    def others_y(self):
        return [self.at(y=(self.y + d) % self.ny) for d in range(1, self.ny)]

    def others_x(self):
        return [((self.x + d) % self.nx, self.at(x=(self.x + d) % self.nx)) for d in range(1, self.nx)]

    def others_hc(self):
        return [self.at(h=(self.h + rel // 2) % 2, c=(self.c + rel % 2) % 2) for rel in (1, 2, 3)]


def greet(devices):
    barrier = pltpu.get_barrier_semaphore()
    for device in devices:
        pl.semaphore_signal(barrier, inc=1, device_id=device, device_id_type=MESH)


def await_greetings(count):
    pl.semaphore_wait(pltpu.get_barrier_semaphore(), count)


def near_mask(near, counts, width):
    blocks, listed = near.shape
    lanes = lax.broadcasted_iota(jnp.int32, (blocks, width), 1)
    mask = jnp.zeros((blocks, width), F32)
    for n in range(listed):
        hit = jnp.where(near[:, n : n + 1] == lanes, 1.0, 0.0)
        mask = mask + jnp.where(counts > n, hit, 0.0)
    return mask


def pair_list(place, row_mask, col_mask):
    z, h, c, x, ny = place.z, place.h, place.c, place.x, place.ny
    sources_x = SOURCES_Y + ny
    rows, cols = row_mask.shape[0], col_mask.shape[0]
    own = rows + cols
    lane = lax.broadcasted_iota(jnp.int32, (128, 128), 0)
    k = lax.broadcasted_iota(jnp.int32, (128, 128), 1)
    rel = k // 4
    from_row = (k // 4) * (NZ * 4) + z * 4 + k % 4
    from_col = x * 16 + ((rel // 2 + h) % 2) * 8 + ((rel + c) % 2) * 4 + k % 4
    bf = jnp.bfloat16
    pick_row = jnp.where((lane == from_row) & (k < ny * 4), 1.0, 0.0).astype(bf)
    pick_col = jnp.where((lane == from_col) & (k < 16), 1.0, 0.0).astype(bf)
    dot = functools.partial(jnp.dot, preferred_element_type=F32)
    live = jnp.concatenate([dot(row_mask.astype(bf), pick_row), dot(col_mask.astype(bf), pick_col)], axis=0)
    before = dot(live.astype(bf), jnp.where(lane < k, 1.0, 0.0).astype(bf))
    totals = jnp.broadcast_to(jnp.sum(live, axis=1, keepdims=True), (own, 128))
    above = lax.broadcasted_iota(jnp.int32, (own, own), 0) > lax.broadcasted_iota(jnp.int32, (own, own), 1)
    offset = dot(jnp.where(above, 1.0, 0.0).astype(bf), totals.astype(bf))
    rank = jnp.where(live > 0.5, before + offset, -1.0)

    a = lax.broadcasted_iota(jnp.int32, (own, 128), 0)
    k = lax.broadcasted_iota(jnp.int32, (own, 128), 1)
    rel = k // 4
    unit = jnp.where(
        rel == 0, z, jnp.where(rel == 1, SIBLING, jnp.where(rel == 2, AHEAD + z % HALF, SIBLING + 1))
    )
    is_row = a < rows
    own_block = jnp.where(is_row, a, a - rows + sources_x * 4)
    far_block = jnp.where(is_row, SOURCES_Y * 4 + k, unit * 4 + k % 4)
    far_slot = jnp.where(is_row, k, ny * 4 + k)
    code = (own_block + 128 * far_block + 16384 * far_slot).astype(F32)

    fill = jnp.zeros((128 - own, 128), F32)
    rank_t = jnp.transpose(jnp.concatenate([rank, fill - 1.0], axis=0))[:16]
    code_t = jnp.transpose(jnp.concatenate([code, fill], axis=0))[:16]
    slots = lax.broadcasted_iota(jnp.int32, (16, 128), 1).astype(F32)
    packed = [jnp.zeros((16, 128), F32) for _ in range(MAX_PAIRS_ROWS)]
    for one in range(own):
        rank_one = jnp.broadcast_to(rank_t[:, one : one + 1], (16, 128))
        code_one = jnp.broadcast_to(code_t[:, one : one + 1], (16, 128))
        for r in range(MAX_PAIRS_ROWS):
            packed[r] = packed[r] + jnp.where(rank_one == slots + 128.0 * r, code_one, 0.0)
    listing = [jnp.sum(part, axis=0, keepdims=True) for part in packed]
    count = jnp.broadcast_to(jnp.sum(jnp.sum(live, axis=1, keepdims=True), axis=0, keepdims=True), (2, 128))
    return jnp.concatenate(listing + [count], axis=0).astype(jnp.int32)


def gather_kernel(
    nx,
    ny,
    source_ref,
    adjoint_ref,
    points_ref,
    near_rows_ref,
    counts_rows_ref,
    near_cols_ref,
    counts_cols_ref,
    blocks_ref,
    meta_ref,
    list_ref,
    own_meta,
    ring_send,
    ring_recv,
    core_send,
    core_recv,
    y_send,
    y_recv,
    x_send,
    x_recv,
    meta_send,
    meta_recv,
    local_sem,
):
    place = Place(nx, ny)
    z, x, y = place.z, place.x, place.y
    per_device = source_ref.shape[0]
    sources_x = SOURCES_Y + ny
    right, left = place.beside(True), place.beside(False)
    sides = (right, left)
    others_z, others_y, others_x, others_hc = (
        place.others_z(),
        place.others_y(),
        place.others_x(),
        place.others_hc(),
    )
    sibling = others_hc[0]
    met = [device for _, device in others_z] + others_y + [device for _, device in others_x] + others_hc
    met = met + [right, left]
    greet(met)

    own_meta[...] = jnp.zeros_like(own_meta)
    row_mask = near_mask(near_rows_ref[...], counts_rows_ref[...], 128)
    col_mask = near_mask(near_cols_ref[...], counts_cols_ref[...], 128)
    for b in range(per_device):
        own_meta[b, 0:3, :] = points_ref[b].astype(F32)
        own_meta[b, 4:5, :] = row_mask[b : b + 1]
        own_meta[b, 5:6, :] = col_mask[b : b + 1]

    await_greetings(len(met))

    def remote(src, dst, send, recv, device):
        return pltpu.make_async_remote_copy(
            src_ref=src, dst_ref=dst, send_sem=send, recv_sem=recv, device_id=device, device_id_type=MESH
        )

    def mirrored(side):
        return z if side == 0 else NZ - 1 - z

    def unit_of(side, m, t):
        near = m - 1 - t
        ahead = 3 - (t - m)
        if side == 0:
            return jnp.where(t < m, near, AHEAD + ahead)
        return jnp.where(t < m, NZ - 1 - near, AHEAD + 3 - ahead)

    def arrivals(m):
        return jnp.where(m < HALF, HALF, m)

    def forwards(m, t):
        last = m == NZ - 1
        return jnp.where(m < HALF, t < HALF - 1, jnp.where(last, t >= HALF - 1, True)) & (t < arrivals(m))

    def sent_unit(side, m, unit):
        crossed = AHEAD + unit if side == 0 else AHEAD + unit - HALF
        return jnp.where(m == NZ - 1, crossed, unit)

    def sent_number(m, t):
        return jnp.where(m == NZ - 1, t - (HALF - 1), t + 1)

    def ring_copy(side, t, b):
        m = mirrored(side)
        unit = unit_of(side, m, t)
        return remote(
            blocks_ref.at[unit, b],
            blocks_ref.at[sent_unit(side, m, unit), b],
            ring_send.at[side, t + 1, b],
            ring_recv.at[side, sent_number(m, t), b],
            sides[side],
        )

    def own_copy(side, b):
        return remote(
            adjoint_ref.at[b],
            blocks_ref.at[z, b],
            ring_send.at[side, 0, b],
            ring_recv.at[side, 0, b],
            sides[side],
        )

    def arrival(side, t, b):
        unit = unit_of(side, mirrored(side), t)
        slot = blocks_ref.at[unit, b]
        return remote(slot, slot, ring_send.at[side, t + 1, b], ring_recv.at[side, t, b], sides[side])

    def core_copy(b):
        return remote(
            blocks_ref.at[AHEAD + z % HALF, b],
            blocks_ref.at[SIBLING + 1, b],
            core_send.at[b],
            core_recv.at[b],
            sibling,
        )

    core_own = remote(
        adjoint_ref, blocks_ref.at[SIBLING], core_send.at[per_device], core_recv.at[per_device], sibling
    )

    for b in range(per_device):
        for side in (0, 1):

            @pl.when(mirrored(side) < NZ - 1)
            def _():
                own_copy(side, b).start()

    metas = []
    own_slots = [z, NZ + x, NZ + nx + y, NZ + nx + ny]
    for d, (_, device) in enumerate(others_z):
        metas.append((own_slots[0], d, device, (z + NZ - 1 - d) % NZ))
    for d, (_, device) in enumerate(others_x):
        metas.append((own_slots[1], NZ + d, device, NZ + (x + nx - 1 - d) % nx))
    for d, device in enumerate(others_y):
        metas.append((own_slots[2], NZ + nx + d, device, NZ + nx + (y + ny - 1 - d) % ny))
    for d, device in enumerate(others_hc):
        metas.append((NZ + nx + ny + 1 + d, NZ + nx + ny + d, device, NZ + nx + ny + 1 + d))
    meta_out = [
        remote(own_meta, meta_ref.at[slot], meta_send.at[s], meta_recv.at[s], device)
        for slot, s, device, _ in metas
    ]
    meta_in = [
        remote(own_meta, meta_ref.at[slot], meta_send.at[s], meta_recv.at[s], device)
        for _, s, device, slot in metas
    ]
    for copy in meta_out:
        copy.start()
    core_own.start()
    y_out, y_in, x_out, x_in = [], [], [], []
    for d, device in enumerate(others_y):
        sems = (y_send.at[d], y_recv.at[d], device)
        y_out.append(remote(source_ref, blocks_ref.at[SOURCES_Y + y], *sems))
        y_in.append(remote(source_ref, blocks_ref.at[SOURCES_Y + (y + ny - 1 - d) % ny], *sems))
    for d, (_, device) in enumerate(others_x):
        sems = (x_send.at[d], x_recv.at[d], device)
        x_out.append(remote(source_ref, blocks_ref.at[sources_x + x], *sems))
        x_in.append(remote(source_ref, blocks_ref.at[sources_x + (x + nx - 1 - d) % nx], *sems))
    for copy in y_out + x_out:
        copy.start()
    locals_ = [
        pltpu.make_async_copy(adjoint_ref, blocks_ref.at[z], local_sem.at[0]),
        pltpu.make_async_copy(source_ref, blocks_ref.at[SOURCES_Y + y], local_sem.at[1]),
        pltpu.make_async_copy(source_ref, blocks_ref.at[sources_x + x], local_sem.at[2]),
    ]
    for copy in locals_:
        copy.start()
    for slot in own_slots:
        meta_ref[slot] = own_meta[...]

    def due(m, hops):
        near = hops < m
        ahead = (m < HALF) & (hops >= HALF + m) & (hops < 2 * HALF)
        return near | ahead, jnp.where(near, hops, hops - HALF)

    def ring_step(s, carry):
        hops, b = s // per_device, s % per_device
        for side in (0, 1):
            m = mirrored(side)
            comes, t = due(m, hops)

            @pl.when(comes)
            def _():
                arrival(side, t, b).wait_recv()

                @pl.when(forwards(m, t))
                def _():
                    ring_copy(side, t, b).start()

                @pl.when((m < HALF) & (t == HALF - 1))
                def _():
                    core_copy(b).start()

        return carry

    lax.fori_loop(0, 2 * per_device, ring_step, 0)

    for copy in meta_in:
        copy.wait_recv()
    tiles = NZ * per_device
    row_masks = jnp.concatenate([meta_ref[u, b, 4:5, :] for u in range(NZ) for b in range(per_device)], axis=0)
    col_masks = jnp.concatenate(
        [meta_ref[NZ + u, b, 5:6, :] for u in range(nx) for b in range(per_device)], axis=0
    )
    list_ref[...] = pair_list(place, row_masks, col_masks)

    lax.fori_loop(2 * per_device, NZ * per_device, ring_step, 0)

    for copy in y_in + x_in:
        copy.wait_recv()
    for b in range(per_device):
        core_copy(b).wait_recv()
    core_own.wait_recv()
    for copy in locals_:
        copy.wait()
    for copy in y_out + x_out + meta_out + [core_own]:
        copy.wait_send()
    for b in range(per_device):
        core_copy(b).wait_send()
        for side in (0, 1):

            @pl.when(mirrored(side) < NZ - 1)
            def _():
                own_copy(side, b).wait_send()

    def sent_step(s, carry):
        t, b = s // per_device, s % per_device
        for side in (0, 1):

            @pl.when(forwards(mirrored(side), t))
            def _():
                ring_copy(side, t, b).wait_send()

        return carry

    lax.fori_loop(0, (NZ - 1) * per_device, sent_step, 0)


UNROLL = 4


def pair_kernel(rows, own, shift, list_ref, blocks_hbm, meta_ref, out_ref, blocks, far_axes, acc, sems):
    units, per_device = blocks_hbm.shape[:2]
    copies = [
        pltpu.make_async_copy(blocks_hbm.at[u], blocks.at[pl.ds(u * per_device, per_device)], sems.at[u])
        for u in range(units)
    ]
    for copy in copies:
        copy.start()
    acc[...] = jnp.zeros_like(acc)
    fars = far_axes.shape[0]
    axis = lax.broadcasted_iota(jnp.int32, (8, 3 * 128), 0)
    wanted = lax.broadcasted_iota(jnp.int32, (8, 3 * 128), 1) // 128
    spread = jnp.where(axis == wanted, 1.0, 0.0)

    def spread_far(j, carry):
        tile = meta_ref[own + j]
        far_axes[j] = lax.dot_general(
            tile, spread, (((0,), (0,)), ((), ())), preferred_element_type=F32, precision=lax.Precision.HIGHEST
        )
        return carry

    lax.fori_loop(0, fars, spread_far, 0)
    for copy in copies:
        copy.wait()
    count = list_ref[MAX_PAIRS_ROWS, 0]

    def one_pair(k):
        code = list_ref[k // 128, k % 128]
        own_block, far_block, far_slot = code & 127, (code >> 7) & 127, code >> 14
        acc_slot = jnp.where(own_block < rows, own_block, own_block - shift)
        weights = lax.dot_general(
            blocks[far_block], blocks[own_block], (((1,), (1,)), ((), ())), preferred_element_type=F32
        )
        tile = meta_ref[acc_slot]
        own_axes = [jnp.broadcast_to(tile[c : c + 1], (8, 128)) for c in range(3)]
        sums = [jnp.zeros((8, 128), F32) for _ in range(3)]
        for r in range(16):
            at = slice(8 * r, 8 * r + 8)
            d = [far_axes[far_slot, at, 128 * c : 128 * c + 128] - own_axes[c] for c in range(3)]
            inverse = lax.rsqrt(d[0] * d[0] + d[1] * d[1] + d[2] * d[2] + EPS2)
            scaled = weights[at] * (inverse * inverse * inverse)
            sums = [sums[c] + d[c] * scaled for c in range(3)]
        return jnp.where(k < count, acc_slot, own), sums

    def step(i, carry):
        done = [one_pair(i * UNROLL + u) for u in range(UNROLL)]
        for slot, sums in done:
            for c in range(3):
                acc[slot, c] = acc[slot, c] + sums[c]
        return carry

    lax.fori_loop(0, (count + UNROLL - 1) // UNROLL, step, 0)
    out_ref[...] = jnp.zeros_like(out_ref)
    for a in range(own):
        for c in range(3):
            out_ref[a // per_device, (a % per_device) * 4 + c : (a % per_device) * 4 + c + 1, :] = jnp.sum(
                acc[a, c], axis=0, keepdims=True
            )


def return_kernel(nx, ny, parts_ref, out_ref, landed, send_sem, recv_sem):
    place = Place(nx, ny)
    z, x = place.z, place.x
    others_z, others_x = place.others_z(), place.others_x()
    met = [device for _, device in others_z] + [device for _, device in others_x]
    greet(met)
    landed[z] = parts_ref[z]
    landed[NZ + x] = parts_ref[NZ + x]
    await_greetings(len(met))
    outgoing, incoming = [], []

    def both(s, theirs, mine, source, device):
        for slot, copies in ((mine, outgoing), (source, incoming)):
            copies.append(
                pltpu.make_async_remote_copy(
                    src_ref=parts_ref.at[theirs],
                    dst_ref=landed.at[slot],
                    send_sem=send_sem.at[s],
                    recv_sem=recv_sem.at[s],
                    device_id=device,
                    device_id_type=MESH,
                )
            )

    for d, (other, device) in enumerate(others_z):
        both(d, other, z, (z + NZ - 1 - d) % NZ, device)
    for d, (other, device) in enumerate(others_x):
        both(NZ + d, NZ + other, NZ + x, NZ + (x + nx - 1 - d) % nx, device)
    for copy in outgoing:
        copy.start()
    for copy in incoming:
        copy.wait_recv()
    total = landed[0]
    for u in range(1, NZ + nx):
        total = total + landed[u]
    for b in range(out_ref.shape[0]):
        out_ref[b] = total[4 * b : 4 * b + 3]
    for copy in outgoing:
        copy.wait_send()


def shards(
    nx,
    ny,
    source_strength,
    adjoint_strength,
    node_points,
    near_rows,
    counts_rows,
    near_cols,
    counts_cols,
):
    _, per_device, size_block, conditions = source_strength.shape
    units = SOURCES_Y + ny + nx
    metas = NZ + nx + ny + 4
    dma = pltpu.SemaphoreType.DMA
    any_space = pl.BlockSpec(memory_space=pl.ANY)
    vmem = pl.BlockSpec(memory_space=pltpu.VMEM)
    blocks, meta, listing = pl.pallas_call(
        functools.partial(gather_kernel, nx, ny),
        name="gather",
        out_shape=(
            jax.ShapeDtypeStruct((units, per_device, size_block, conditions), jnp.bfloat16),
            jax.ShapeDtypeStruct((metas, per_device, 8, 128), F32),
            jax.ShapeDtypeStruct((8, 128), jnp.int32),
        ),
        in_specs=[any_space, any_space] + [vmem] * 5,
        out_specs=(any_space, vmem, vmem),
        scratch_shapes=[
            pltpu.VMEM((per_device, 8, 128), F32),
            dma((2, NZ, per_device)),
            dma((2, NZ, per_device)),
            dma((per_device + 1,)),
            dma((per_device + 1,)),
            dma((max(ny - 1, 1),)),
            dma((max(ny - 1, 1),)),
            dma((max(nx - 1, 1),)),
            dma((max(nx - 1, 1),)),
            dma((metas,)),
            dma((metas,)),
            dma((3,)),
        ],
        compiler_params=pltpu.CompilerParams(
            collective_id=0, has_side_effects=True, vmem_limit_bytes=16 * 1024 * 1024
        ),
    )(
        source_strength[0],
        adjoint_strength[0],
        node_points[0],
        near_rows[0],
        counts_rows[0][:, None],
        near_cols[0],
        counts_cols[0][:, None],
    )
    rows = NZ * per_device
    own = rows + nx * per_device
    fars = (ny + 4) * per_device
    shift = (SOURCES_Y + ny) * per_device - rows
    parts = pl.pallas_call(
        functools.partial(pair_kernel, rows, own, shift),
        name="pairs",
        out_shape=jax.ShapeDtypeStruct((NZ + nx, 4 * per_device, 128), F32),
        in_specs=[pl.BlockSpec(memory_space=pltpu.SMEM), any_space, vmem],
        out_specs=vmem,
        scratch_shapes=[
            pltpu.VMEM((units * per_device, size_block, conditions), jnp.bfloat16),
            pltpu.VMEM((fars, 128, 3 * 128), F32),
            pltpu.VMEM((own + 1, 3, 8, 128), F32),
            dma((units,)),
        ],
        compiler_params=pltpu.CompilerParams(vmem_limit_bytes=32 * 1024 * 1024),
    )(listing, blocks, meta.reshape(metas * per_device, 8, 128))
    total = pl.pallas_call(
        functools.partial(return_kernel, nx, ny),
        name="sums",
        out_shape=jax.ShapeDtypeStruct((per_device, 3, 128), F32),
        in_specs=[vmem],
        out_specs=vmem,
        scratch_shapes=[
            pltpu.VMEM((NZ + nx, 4 * per_device, 128), F32),
            dma((NZ + nx,)),
            dma((NZ + nx,)),
        ],
        compiler_params=pltpu.CompilerParams(collective_id=1, has_side_effects=True),
    )(parts)
    return total[None]


def solution(mesh):
    nx, ny = mesh.shape["blk"] // 4, mesh.shape["wide"] // NZ
    return jax.shard_map(
        functools.partial(shards, nx, ny),
        mesh=mesh,
        in_specs=(
            P("blk", "wide", None, None),
            P("blk", "wide", None, None),
            P("blk", "wide", None, None),
            P("blk", "wide", None),
            P("blk", "wide"),
            P("blk", "wide", None),
            P("blk", "wide"),
        ),
        out_specs=P("blk", "wide", None, None),
        check_vma=False,
    )
```

time: 504 us -> 106 us (0.21)
  the two profiles are of different devices: /device:TPU:4 before, /device:TPU:1 now
where the time goes in v1:
time: 106 us; the launch traced here: 105 us
  Pallas kernels  98.1 us (93%)
  local copies, waits for them, and re-layouts  7.35 us (7%)
    pallas_call x1, Pallas kernels, shards(): pl.pallas_call(functools.partial(gather_kernel, nx, ny), name='gather', o...  68 us
    pallas_call x1, Pallas kernels, shards(): pl.pallas_call(functools.partial(pair_kernel, rows, own, shift), name='pa...  15.7 us
    pallas_call x1, Pallas kernels, shards(): pl.pallas_call(functools.partial(return_kernel, nx, ny), name='sums', out...  14.4 us
    unnamed x11, local copies, waits for them, and re-layouts  4.57 us

profile of v1, /device:TPU:1, one launch (start us, length us, event | category | flops | bytes accessed | tf_op | source)
XLA Modules:
  0.0 105.5 jit_solution(781471887796444451)
XLA Ops:
  0.0 0.7 copy.9.counts_rows_ref
  0.7 0.7 copy.10.counts_cols_ref
  1.5 0.7 copy.13
  2.2 0.0 copy-start.1
  2.2 0.9 copy-done.1
  3.1 0.0 copy-start.2
  3.1 0.9 copy-done.2
  4.1 0.0 copy-start.3
  4.1 0.7 copy-done.3
  4.8 0.0 copy-start.4
  4.8 0.7 copy-done.4
  5.4 68.0 %gather.1 = (bf16[22,4,128,256]{3,2,1,0:T(8,128)(2,1)S(1)}, f32[20,4,8,128]{3,2,1,0:T(8,128)S(1)}, s32[8,128]{1,0:T(8,128)S(1)}) custom-call(bf16[4,128,256]{2,1,0:T(8,128)(2,1)S(1)} %bitcast.12, bf16[4,128,256]{2,1,0:T(8,128)(2,1)S(1)} %bitcast.13, bf16[4,3,128]{2,1,0:T(4,128)(2,1)S(1)} %bitcast.14, s32[4,32]{1,0:T(4,128)S(1)} %bitcast.15, ...), custom_call_target="tpu_custom_call" | custom-call | tf_op jit(solution)/shard_map/gather/pallas_call | solution.py:483
  73.5 15.7 %pairs.1.parts_ref = f32[12,16,128]{2,1,0:T(8,128)S(1)} custom-call(s32[8,128]{1,0:T(8,128)S(1)} %get-tuple-element.8.list_ref, bf16[22,4,128,256]{3,2,1,0:T(8,128)(2,1)S(1)} %get-tuple-element.9.blocks_hbm, f32[80,8,128]{2,1,0:T(8,128)S(1)} %bitcast.11), custom_call_target="tpu_custom_call" | custom-call | tf_op jit(solution)/shard_map/pairs/pallas_call | solution.py:523
  89.2 0.0 copy-start
  89.2 0.6 copy-done
  89.8 14.4 %sums.1 = f32[4,3,128]{2,1,0:T(4,128)} custom-call(f32[12,16,128]{2,1,0:T(8,128)} %copy-done), custom_call_target="tpu_custom_call" | custom-call | tf_op jit(solution)/shard_map/sums/pallas_call | solution.py:537
  104.2 1.3 %copy.11 = f32[1,4,3,128]{3,1,2,0:T(4,128)} copy(f32[1,4,3,128]{3,2,1,0:T(4,128)} %bitcast.17) | data formatting | bytes 12288 | tf_op jit(solution)/shard_map/broadcast_in_dim | solution.py:550
Async XLA Ops:
  2.2 0.9 copy-start.1
  3.1 0.9 copy-start.2
  4.1 0.7 copy-start.3
  4.8 0.7 copy-start.4
  89.2 0.6 copy-start

commit v2 on v1

--- a/solution.py
+++ b/solution.py
@@ -17,6 +17,7 @@
 SIBLING = AHEAD + HALF
 SOURCES_Y = SIBLING + 2
 MAX_PAIRS_ROWS = 6
+SPLIT = 1
 
 
 class Place:
@@ -66,6 +67,9 @@
 
 def near_mask(near, counts, width):
     blocks, listed = near.shape
+    row = lax.broadcasted_iota(jnp.int32, (blocks, blocks), 0)
+    own = row == lax.broadcasted_iota(jnp.int32, (blocks, blocks), 1)
+    counts = jnp.sum(jnp.where(own, jnp.broadcast_to(counts, (blocks, blocks)), 0), axis=1, keepdims=True)
     lanes = lax.broadcasted_iota(jnp.int32, (blocks, width), 1)
     mask = jnp.zeros((blocks, width), F32)
     for n in range(listed):
@@ -127,14 +131,20 @@
     ny,
     source_ref,
     adjoint_ref,
+    points_hbm,
+    near_rows_hbm,
+    counts_rows_hbm,
+    near_cols_hbm,
+    counts_cols_hbm,
+    blocks_ref,
+    meta_ref,
+    far_axes_ref,
+    list_ref,
     points_ref,
     near_rows_ref,
     counts_rows_ref,
     near_cols_ref,
     counts_cols_ref,
-    blocks_ref,
-    meta_ref,
-    list_ref,
     own_meta,
     ring_send,
     ring_recv,
@@ -147,7 +157,22 @@
     meta_send,
     meta_recv,
     local_sem,
+    small_sem,
 ):
+    smalls = [
+        pltpu.make_async_copy(src, dst, small_sem.at[i])
+        for i, (src, dst) in enumerate(
+            (
+                (points_hbm, points_ref),
+                (near_rows_hbm, near_rows_ref),
+                (counts_rows_hbm, counts_rows_ref),
+                (near_cols_hbm, near_cols_ref),
+                (counts_cols_hbm, counts_cols_ref),
+            )
+        )
+    ]
+    for copy in smalls:
+        copy.start()
     place = Place(nx, ny)
     z, x, y = place.z, place.x, place.y
     per_device = source_ref.shape[0]
@@ -165,11 +190,15 @@
     met = met + [right, left]
     greet(met)
 
+    for copy in smalls:
+        copy.wait()
     own_meta[...] = jnp.zeros_like(own_meta)
     row_mask = near_mask(near_rows_ref[...], counts_rows_ref[...], 128)
     col_mask = near_mask(near_cols_ref[...], counts_cols_ref[...], 128)
+    points = [points_ref[c].astype(F32) for c in range(3)]
     for b in range(per_device):
-        own_meta[b, 0:3, :] = points_ref[b].astype(F32)
+        for c in range(3):
+            own_meta[b, c : c + 1, :] = points[c][b : b + 1]
         own_meta[b, 4:5, :] = row_mask[b : b + 1]
         own_meta[b, 5:6, :] = col_mask[b : b + 1]
 
@@ -204,12 +233,18 @@
     def sent_number(m, t):
         return jnp.where(m == NZ - 1, t - (HALF - 1), t + 1)
 
+    chunks = per_device * SPLIT
+    depth = source_ref.shape[1] // SPLIT
+
+    def part(ref, s):
+        return ref.at[s // SPLIT, pl.ds(s % SPLIT * depth, depth)]
+
     def ring_copy(side, t, b):
         m = mirrored(side)
         unit = unit_of(side, m, t)
         return remote(
-            blocks_ref.at[unit, b],
-            blocks_ref.at[sent_unit(side, m, unit), b],
+            part(blocks_ref.at[unit], b),
+            part(blocks_ref.at[sent_unit(side, m, unit)], b),
             ring_send.at[side, t + 1, b],
             ring_recv.at[side, sent_number(m, t), b],
             sides[side],
@@ -217,8 +252,8 @@
 
     def own_copy(side, b):
         return remote(
-            adjoint_ref.at[b],
-            blocks_ref.at[z, b],
+            part(adjoint_ref, b),
+            part(blocks_ref.at[z], b),
             ring_send.at[side, 0, b],
             ring_recv.at[side, 0, b],
             sides[side],
@@ -226,23 +261,23 @@
 
     def arrival(side, t, b):
         unit = unit_of(side, mirrored(side), t)
-        slot = blocks_ref.at[unit, b]
+        slot = part(blocks_ref.at[unit], b)
         return remote(slot, slot, ring_send.at[side, t + 1, b], ring_recv.at[side, t, b], sides[side])
 
     def core_copy(b):
         return remote(
-            blocks_ref.at[AHEAD + z % HALF, b],
-            blocks_ref.at[SIBLING + 1, b],
+            part(blocks_ref.at[AHEAD + z % HALF], b),
+            part(blocks_ref.at[SIBLING + 1], b),
             core_send.at[b],
             core_recv.at[b],
             sibling,
         )
 
     core_own = remote(
-        adjoint_ref, blocks_ref.at[SIBLING], core_send.at[per_device], core_recv.at[per_device], sibling
+        adjoint_ref, blocks_ref.at[SIBLING], core_send.at[chunks], core_recv.at[chunks], sibling
     )
 
-    for b in range(per_device):
+    for b in range(chunks):
         for side in (0, 1):
 
             @pl.when(mirrored(side) < NZ - 1)
@@ -297,7 +332,7 @@
         return near | ahead, jnp.where(near, hops, hops - HALF)
 
     def ring_step(s, carry):
-        hops, b = s // per_device, s % per_device
+        hops, b = s // chunks, s % chunks
         for side in (0, 1):
             m = mirrored(side)
             comes, t = due(m, hops)
@@ -316,29 +351,53 @@
 
         return carry
 
-    lax.fori_loop(0, 2 * per_device, ring_step, 0)
+    lax.fori_loop(0, 2 * chunks, ring_step, 0)
 
     for copy in meta_in:
         copy.wait_recv()
-    tiles = NZ * per_device
     row_masks = jnp.concatenate([meta_ref[u, b, 4:5, :] for u in range(NZ) for b in range(per_device)], axis=0)
     col_masks = jnp.concatenate(
         [meta_ref[NZ + u, b, 5:6, :] for u in range(nx) for b in range(per_device)], axis=0
     )
     list_ref[...] = pair_list(place, row_masks, col_masks)
 
-    lax.fori_loop(2 * per_device, NZ * per_device, ring_step, 0)
+    fars = far_axes_ref.shape[0]
+    first_far = NZ + nx
+    steps = (NZ - 2) * chunks
+    each = -(-fars // steps)
+    axis = lax.broadcasted_iota(jnp.int32, (8, 3 * 128), 0)
+    wanted = lax.broadcasted_iota(jnp.int32, (8, 3 * 128), 1) // 128
+    spread = jnp.where(axis == wanted, 1.0, 0.0).astype(jnp.bfloat16)
+
+    def spread_far(j):
+        tile = meta_ref[first_far + j // per_device, j % per_device].astype(jnp.bfloat16)
+        far_axes_ref[j] = lax.dot_general(
+            tile, spread, (((0,), (0,)), ((), ())), preferred_element_type=F32
+        )
+
+    def ring_step_and_far(s, carry):
+        ring_step(s, carry)
+        for e in range(each):
+            j = (s - 2 * chunks) * each + e
+
+            @pl.when(j < fars)
+            def _():
+                spread_far(j)
+
+        return carry
+
+    lax.fori_loop(2 * chunks, NZ * chunks, ring_step_and_far, 0)
 
     for copy in y_in + x_in:
         copy.wait_recv()
-    for b in range(per_device):
+    for b in range(chunks):
         core_copy(b).wait_recv()
     core_own.wait_recv()
     for copy in locals_:
         copy.wait()
     for copy in y_out + x_out + meta_out + [core_own]:
         copy.wait_send()
-    for b in range(per_device):
+    for b in range(chunks):
         core_copy(b).wait_send()
         for side in (0, 1):
 
@@ -347,7 +406,7 @@
                 own_copy(side, b).wait_send()
 
     def sent_step(s, carry):
-        t, b = s // per_device, s % per_device
+        t, b = s // chunks, s % chunks
         for side in (0, 1):
 
             @pl.when(forwards(mirrored(side), t))
@@ -356,36 +415,15 @@
 
         return carry
 
-    lax.fori_loop(0, (NZ - 1) * per_device, sent_step, 0)
+    lax.fori_loop(0, (NZ - 1) * chunks, sent_step, 0)
 
 
 UNROLL = 4
 
 
-def pair_kernel(rows, own, shift, list_ref, blocks_hbm, meta_ref, out_ref, blocks, far_axes, acc, sems):
-    units, per_device = blocks_hbm.shape[:2]
-    copies = [
-        pltpu.make_async_copy(blocks_hbm.at[u], blocks.at[pl.ds(u * per_device, per_device)], sems.at[u])
-        for u in range(units)
-    ]
-    for copy in copies:
-        copy.start()
+def pair_kernel(rows, own, shift, list_ref, blocks, meta_ref, far_axes, out_ref, acc):
+    per_device = out_ref.shape[1] // 4
     acc[...] = jnp.zeros_like(acc)
-    fars = far_axes.shape[0]
-    axis = lax.broadcasted_iota(jnp.int32, (8, 3 * 128), 0)
-    wanted = lax.broadcasted_iota(jnp.int32, (8, 3 * 128), 1) // 128
-    spread = jnp.where(axis == wanted, 1.0, 0.0)
-
-    def spread_far(j, carry):
-        tile = meta_ref[own + j]
-        far_axes[j] = lax.dot_general(
-            tile, spread, (((0,), (0,)), ((), ())), preferred_element_type=F32, precision=lax.Precision.HIGHEST
-        )
-        return carry
-
-    lax.fori_loop(0, fars, spread_far, 0)
-    for copy in copies:
-        copy.wait()
     count = list_ref[MAX_PAIRS_ROWS, 0]
 
     def one_pair(k):
@@ -417,9 +455,8 @@
     out_ref[...] = jnp.zeros_like(out_ref)
     for a in range(own):
         for c in range(3):
-            out_ref[a // per_device, (a % per_device) * 4 + c : (a % per_device) * 4 + c + 1, :] = jnp.sum(
-                acc[a, c], axis=0, keepdims=True
-            )
+            row = c * per_device + a % per_device
+            out_ref[a // per_device, row : row + 1, :] = jnp.sum(acc[a, c], axis=0, keepdims=True)
 
 
 def return_kernel(nx, ny, parts_ref, out_ref, landed, send_sem, recv_sem):
@@ -457,8 +494,9 @@
     total = landed[0]
     for u in range(1, NZ + nx):
         total = total + landed[u]
-    for b in range(out_ref.shape[0]):
-        out_ref[b] = total[4 * b : 4 * b + 3]
+    per_device = out_ref.shape[1]
+    for c in range(3):
+        out_ref[c] = total[c * per_device : (c + 1) * per_device]
     for copy in outgoing:
         copy.wait_send()
 
@@ -479,23 +517,32 @@
     metas = NZ + nx + ny + 4
     dma = pltpu.SemaphoreType.DMA
     any_space = pl.BlockSpec(memory_space=pl.ANY)
+    hbm = pl.BlockSpec(memory_space=pltpu.HBM)
+    fars = (ny + 4) * per_device
+    small = pltpu.CompilerParams(vmem_limit_bytes=8 * 1024 * 1024)
     vmem = pl.BlockSpec(memory_space=pltpu.VMEM)
-    blocks, meta, listing = pl.pallas_call(
+    blocks, meta, far_axes, listing = pl.pallas_call(
         functools.partial(gather_kernel, nx, ny),
         name="gather",
         out_shape=(
             jax.ShapeDtypeStruct((units, per_device, size_block, conditions), jnp.bfloat16),
             jax.ShapeDtypeStruct((metas, per_device, 8, 128), F32),
+            jax.ShapeDtypeStruct((fars, size_block, 3 * 128), F32),
             jax.ShapeDtypeStruct((8, 128), jnp.int32),
         ),
-        in_specs=[any_space, any_space] + [vmem] * 5,
-        out_specs=(any_space, vmem, vmem),
+        in_specs=[hbm] * 7,
+        out_specs=(any_space, vmem, vmem, vmem),
         scratch_shapes=[
+            pltpu.VMEM((3, per_device, size_block), jnp.bfloat16),
+            pltpu.VMEM((per_device, near_rows.shape[2]), jnp.int32),
+            pltpu.VMEM((1, per_device), jnp.int32),
+            pltpu.VMEM((per_device, near_cols.shape[2]), jnp.int32),
+            pltpu.VMEM((1, per_device), jnp.int32),
             pltpu.VMEM((per_device, 8, 128), F32),
-            dma((2, NZ, per_device)),
-            dma((2, NZ, per_device)),
-            dma((per_device + 1,)),
-            dma((per_device + 1,)),
+            dma((2, NZ, per_device * SPLIT)),
+            dma((2, NZ, per_device * SPLIT)),
+            dma((per_device * SPLIT + 1,)),
+            dma((per_device * SPLIT + 1,)),
             dma((max(ny - 1, 1),)),
             dma((max(ny - 1, 1),)),
             dma((max(nx - 1, 1),)),
@@ -503,41 +550,46 @@
             dma((metas,)),
             dma((metas,)),
             dma((3,)),
+            dma((5,)),
         ],
         compiler_params=pltpu.CompilerParams(
             collective_id=0, has_side_effects=True, vmem_limit_bytes=16 * 1024 * 1024
         ),
     )(
-        source_strength[0],
-        adjoint_strength[0],
-        node_points[0],
-        near_rows[0],
-        counts_rows[0][:, None],
-        near_cols[0],
-        counts_cols[0][:, None],
+        *(
+            pltpu.with_memory_space_constraint(operand, pltpu.HBM)
+            for operand in (
+                source_strength[0],
+                adjoint_strength[0],
+                jnp.transpose(node_points[0], (1, 0, 2)),
+                near_rows[0],
+                counts_rows,
+                near_cols[0],
+                counts_cols,
+            )
+        )
     )
     rows = NZ * per_device
     own = rows + nx * per_device
-    fars = (ny + 4) * per_device
     shift = (SOURCES_Y + ny) * per_device - rows
     parts = pl.pallas_call(
         functools.partial(pair_kernel, rows, own, shift),
         name="pairs",
         out_shape=jax.ShapeDtypeStruct((NZ + nx, 4 * per_device, 128), F32),
-        in_specs=[pl.BlockSpec(memory_space=pltpu.SMEM), any_space, vmem],
+        in_specs=[pl.BlockSpec(memory_space=pltpu.SMEM), vmem, vmem, vmem],
         out_specs=vmem,
-        scratch_shapes=[
-            pltpu.VMEM((units * per_device, size_block, conditions), jnp.bfloat16),
-            pltpu.VMEM((fars, 128, 3 * 128), F32),
-            pltpu.VMEM((own + 1, 3, 8, 128), F32),
-            dma((units,)),
-        ],
-        compiler_params=pltpu.CompilerParams(vmem_limit_bytes=32 * 1024 * 1024),
-    )(listing, blocks, meta.reshape(metas * per_device, 8, 128))
+        scratch_shapes=[pltpu.VMEM((own + 1, 3, 8, 128), F32)],
+        compiler_params=small,
+    )(
+        listing,
+        blocks.reshape(units * per_device, size_block, conditions),
+        meta.reshape(metas * per_device, 8, 128),
+        far_axes,
+    )
     total = pl.pallas_call(
         functools.partial(return_kernel, nx, ny),
         name="sums",
-        out_shape=jax.ShapeDtypeStruct((per_device, 3, 128), F32),
+        out_shape=jax.ShapeDtypeStruct((3, per_device, 128), F32),
         in_specs=[vmem],
         out_specs=vmem,
         scratch_shapes=[
@@ -545,9 +597,11 @@
             dma((NZ + nx,)),
             dma((NZ + nx,)),
         ],
-        compiler_params=pltpu.CompilerParams(collective_id=1, has_side_effects=True),
+        compiler_params=pltpu.CompilerParams(
+            collective_id=1, has_side_effects=True, vmem_limit_bytes=8 * 1024 * 1024
+        ),
     )(parts)
-    return total[None]
+    return jnp.transpose(total, (1, 0, 2))[None]
 
 
 def solution(mesh):

time: 106 us -> 87.1 us (0.82)
  Pallas kernels: 98.1 us -> 85.8 us
  local copies, waits for them, and re-layouts: 7.35 us -> 0.6 us
    pallas_call x1, Pallas kernels: 15.7 us -> 4.97 us  [shards(): pl.pallas_call(functools.partial(pair_kernel, rows, own, shift), name='pa...]
    unnamed x11 -> x1, local copies, waits for them, and re-layouts: 4.57 us -> 0.6 us
    pallas_call x1, Pallas kernels: 14.4 us -> 12.6 us  [shards(): pl.pallas_call(functools.partial(return_kernel, nx, ny), name='sums', out...]
    another operation x2 -> x0, local copies, waits for them, and re-layouts: 1.48 us -> none  [the longest x1 0.74 us: shards(): counts_rows[0][:, None]]
    broadcast_in_dim x1 -> x0, local copies, waits for them, and re-layouts: 1.29 us -> none  [shards(): return total[None]]
where the time goes in v2:
time: 87.1 us; the launch traced here: 86.4 us
  Pallas kernels  85.8 us (99%)
    pallas_call x1, Pallas kernels, shards(): pl.pallas_call(functools.partial(gather_kernel, nx, ny), name='gather', o...  68.3 us
    pallas_call x1, Pallas kernels, shards(): pl.pallas_call(functools.partial(return_kernel, nx, ny), name='sums', out...  12.6 us
    pallas_call x1, Pallas kernels, shards(): pl.pallas_call(functools.partial(pair_kernel, rows, own, shift), name='pa...  4.97 us

profile of v2, /device:TPU:1, one launch (start us, length us, event | category | flops | bytes accessed | tf_op | source)
XLA Modules:
  0.0 86.4 jit_solution(5793536179295905669)
XLA Ops:
  0.0 68.3 %gather.1 = (bf16[22,4,128,256]{3,2,1,0:T(8,128)(2,1)S(1)}, f32[20,4,8,128]{3,2,1,0:T(8,128)S(1)}, f32[32,128,384]{2,1,0:T(8,128)S(1)}, s32[8,128]{1,0:T(8,128)S(1)}) custom-call(bf16[4,128,256]{2,1,0:T(8,128)(2,1)} %bitcast.15, bf16[4,128,256]{2,1,0:T(8,128)(2,1)} %bitcast.16, bf16[3,4,128]{2,1,0:T(4,128)(2,1)} %bitcast.17, s32[4,32]{1,0:T(4,128)} %bitcast.18, ...), custom_call_target="tpu_custom_call" | custom-call | tf_op jit(solution)/shard_map/gather/pallas_call | solution.py:524
  68.3 5.0 %pairs.1.parts_ref = f32[12,16,128]{2,1,0:T(8,128)S(1)} custom-call(s32[8,128]{1,0:T(8,128)S(1)} %get-tuple-element.9.list_ref, bf16[88,128,256]{2,1,0:T(8,128)(2,1)S(1)} %bitcast.12, f32[80,8,128]{2,1,0:T(8,128)S(1)} %bitcast.13, f32[32,128,384]{2,1,0:T(8,128)S(1)} %get-tuple-element.12.far_axes), custom_call_target="tpu_custom_call" | custom-call | tf_op jit(solution)/shard_map/pairs/pallas_call | solution.py:575
  73.3 12.6 %sums.1 = f32[3,4,128]{2,1,0:T(4,128)S(1)} custom-call(f32[12,16,128]{2,1,0:T(8,128)S(1)} %pairs.1.parts_ref), custom_call_target="tpu_custom_call" | custom-call | tf_op jit(solution)/shard_map/sums/pallas_call | solution.py:589
  85.8 0.6 copy.9

commit v3 on v2

--- a/solution.py
+++ b/solution.py
@@ -18,6 +18,8 @@
 SOURCES_Y = SIBLING + 2
 MAX_PAIRS_ROWS = 6
 SPLIT = 1
+MET_AT = 8
+LISTED_AT = 28, 28
 
 
 class Place:
@@ -137,7 +139,7 @@
     near_cols_hbm,
     counts_cols_hbm,
     blocks_ref,
-    meta_ref,
+    own_axes_ref,
     far_axes_ref,
     list_ref,
     points_ref,
@@ -146,8 +148,11 @@
     near_cols_ref,
     counts_cols_ref,
     own_meta,
-    ring_send,
-    ring_recv,
+    meta_ref,
+    through_send,
+    through_recv,
+    extra_send,
+    extra_recv,
     core_send,
     core_recv,
     y_send,
@@ -192,15 +197,11 @@
 
     for copy in smalls:
         copy.wait()
-    own_meta[...] = jnp.zeros_like(own_meta)
+    points = points_ref[...].astype(F32).reshape(3 * per_device, 128)
     row_mask = near_mask(near_rows_ref[...], counts_rows_ref[...], 128)
     col_mask = near_mask(near_cols_ref[...], counts_cols_ref[...], 128)
-    points = [points_ref[c].astype(F32) for c in range(3)]
-    for b in range(per_device):
-        for c in range(3):
-            own_meta[b, c : c + 1, :] = points[c][b : b + 1]
-        own_meta[b, 4:5, :] = row_mask[b : b + 1]
-        own_meta[b, 5:6, :] = col_mask[b : b + 1]
+    for which, mask in enumerate((row_mask, col_mask)):
+        own_meta[which] = jnp.concatenate([points, mask], axis=0).astype(jnp.bfloat16)
 
     await_greetings(len(met))
 
@@ -209,60 +210,62 @@
             src_ref=src, dst_ref=dst, send_sem=send, recv_sem=recv, device_id=device, device_id_type=MESH
         )
 
+    chunks = per_device * SPLIT
+    depth = source_ref.shape[1] // SPLIT
+    hop = 3 * chunks // 4
+
+    def part(ref, s):
+        return ref.at[s // SPLIT, pl.ds(s % SPLIT * depth, depth)]
+
     def mirrored(side):
         return z if side == 0 else NZ - 1 - z
 
-    def unit_of(side, m, t):
-        near = m - 1 - t
-        ahead = 3 - (t - m)
-        if side == 0:
-            return jnp.where(t < m, near, AHEAD + ahead)
-        return jnp.where(t < m, NZ - 1 - near, AHEAD + 3 - ahead)
-
-    def arrivals(m):
-        return jnp.where(m < HALF, HALF, m)
-
-    def forwards(m, t):
-        last = m == NZ - 1
-        return jnp.where(m < HALF, t < HALF - 1, jnp.where(last, t >= HALF - 1, True)) & (t < arrivals(m))
-
-    def sent_unit(side, m, unit):
+    def slot_of(side, unit):
+        return unit if side == 0 else NZ - 1 - unit
+
+    def through_unit(side, m, t):
+        near = jnp.where(m < HALF, m - 1 - t, HALF - 1 - t)
+        ahead = HALF - 1 - (t - m)
+        is_near = (m >= HALF) | (t < m)
+        return jnp.where(is_near, slot_of(side, near), AHEAD + (ahead if side == 0 else HALF - 1 - ahead))
+
+    def passes_on(m, t):
+        return (m >= HALF) | (t < HALF - 1)
+
+    def through_copy(side, t, b):
+        m = mirrored(side)
+        unit = through_unit(side, m, t)
         crossed = AHEAD + unit if side == 0 else AHEAD + unit - HALF
-        return jnp.where(m == NZ - 1, crossed, unit)
-
-    def sent_number(m, t):
-        return jnp.where(m == NZ - 1, t - (HALF - 1), t + 1)
-
-    chunks = per_device * SPLIT
-    depth = source_ref.shape[1] // SPLIT
-
-    def part(ref, s):
-        return ref.at[s // SPLIT, pl.ds(s % SPLIT * depth, depth)]
-
-    def ring_copy(side, t, b):
-        m = mirrored(side)
-        unit = unit_of(side, m, t)
         return remote(
             part(blocks_ref.at[unit], b),
-            part(blocks_ref.at[sent_unit(side, m, unit)], b),
-            ring_send.at[side, t + 1, b],
-            ring_recv.at[side, sent_number(m, t), b],
+            part(blocks_ref.at[jnp.where(m == NZ - 1, crossed, unit)], b),
+            through_send.at[side, t + 1, b],
+            through_recv.at[side, jnp.where(m < HALF, t + 1, t), b],
             sides[side],
         )
 
+    def through_arrival(side, t, b):
+        slot = part(blocks_ref.at[through_unit(side, mirrored(side), t)], b)
+        return remote(slot, slot, through_send.at[side, t + 1, b], through_recv.at[side, t, b], sides[side])
+
+    def extra_copy(side, e, b):
+        slot = part(blocks_ref.at[slot_of(side, mirrored(side) - 1 - e)], b)
+        return remote(slot, slot, extra_send.at[side, e + 1, b], extra_recv.at[side, e + 1, b], sides[side])
+
+    def extra_arrival(side, e, b):
+        slot = part(blocks_ref.at[slot_of(side, mirrored(side) - 1 - e)], b)
+        return remote(slot, slot, extra_send.at[side, e + 1, b], extra_recv.at[side, e, b], sides[side])
+
     def own_copy(side, b):
-        return remote(
-            part(adjoint_ref, b),
-            part(blocks_ref.at[z], b),
-            ring_send.at[side, 0, b],
-            ring_recv.at[side, 0, b],
-            sides[side],
-        )
-
-    def arrival(side, t, b):
-        unit = unit_of(side, mirrored(side), t)
-        slot = part(blocks_ref.at[unit], b)
-        return remote(slot, slot, ring_send.at[side, t + 1, b], ring_recv.at[side, t, b], sides[side])
+        send, recv = through_send.at[side, 0, b], through_recv.at[side, 0, b]
+        return remote(part(adjoint_ref, b), part(blocks_ref.at[z], b), send, recv, sides[side])
+
+    def own_extra_copy(side, b):
+        send, recv = extra_send.at[side, 0, b], extra_recv.at[side, 0, b]
+        return remote(part(adjoint_ref, b), part(blocks_ref.at[z], b), send, recv, sides[side])
+
+    def sends_extra(m):
+        return (m >= HALF) & (m < NZ - 1)
 
     def core_copy(b):
         return remote(
@@ -279,28 +282,33 @@
 
     for b in range(chunks):
         for side in (0, 1):
-
-            @pl.when(mirrored(side) < NZ - 1)
+            m = mirrored(side)
+
+            @pl.when(m < HALF)
             def _():
                 own_copy(side, b).start()
+
+            @pl.when(sends_extra(m) & ((m > HALF) | (b < hop)))
+            def _():
+                own_extra_copy(side, b).start()
 
     metas = []
     own_slots = [z, NZ + x, NZ + nx + y, NZ + nx + ny]
     for d, (_, device) in enumerate(others_z):
-        metas.append((own_slots[0], d, device, (z + NZ - 1 - d) % NZ))
+        metas.append((0, own_slots[0], d, device, (z + NZ - 1 - d) % NZ))
     for d, (_, device) in enumerate(others_x):
-        metas.append((own_slots[1], NZ + d, device, NZ + (x + nx - 1 - d) % nx))
+        metas.append((1, own_slots[1], NZ + d, device, NZ + (x + nx - 1 - d) % nx))
     for d, device in enumerate(others_y):
-        metas.append((own_slots[2], NZ + nx + d, device, NZ + nx + (y + ny - 1 - d) % ny))
+        metas.append((1, own_slots[2], NZ + nx + d, device, NZ + nx + (y + ny - 1 - d) % ny))
     for d, device in enumerate(others_hc):
-        metas.append((NZ + nx + ny + 1 + d, NZ + nx + ny + d, device, NZ + nx + ny + 1 + d))
+        metas.append((1, NZ + nx + ny + 1 + d, NZ + nx + ny + d, device, NZ + nx + ny + 1 + d))
     meta_out = [
-        remote(own_meta, meta_ref.at[slot], meta_send.at[s], meta_recv.at[s], device)
-        for slot, s, device, _ in metas
+        remote(own_meta.at[which], meta_ref.at[slot], meta_send.at[s], meta_recv.at[s], device)
+        for which, slot, s, device, _ in metas
     ]
     meta_in = [
-        remote(own_meta, meta_ref.at[slot], meta_send.at[s], meta_recv.at[s], device)
-        for _, s, device, slot in metas
+        remote(own_meta.at[which], meta_ref.at[slot], meta_send.at[s], meta_recv.at[s], device)
+        for which, _, s, device, slot in metas
     ]
     for copy in meta_out:
         copy.start()
@@ -323,70 +331,110 @@
     ]
     for copy in locals_:
         copy.start()
-    for slot in own_slots:
-        meta_ref[slot] = own_meta[...]
-
-    def due(m, hops):
-        near = hops < m
-        ahead = (m < HALF) & (hops >= HALF + m) & (hops < 2 * HALF)
-        return near | ahead, jnp.where(near, hops, hops - HALF)
+    for which, slot in zip((0, 1, 1, 1), own_slots):
+        meta_ref[slot] = own_meta[which]
 
     def ring_step(s, carry):
-        hops, b = s // chunks, s % chunks
         for side in (0, 1):
             m = mirrored(side)
-            comes, t = due(m, hops)
+            far = s - hop * (m - HALF + 1)
+            near = s - hop
+            ahead = s - hop * (HALF + 1) + (chunks - hop) * m
+            is_near = near < chunks * m
+            q = jnp.where(m >= HALF, far, jnp.where(is_near, near, ahead))
+            comes = (q >= 0) & (q < HALF * chunks) & ((m >= HALF) | is_near | (ahead >= chunks * m))
+            t, b = jnp.maximum(q, 0) // chunks, jnp.maximum(q, 0) % chunks
 
             @pl.when(comes)
             def _():
-                arrival(side, t, b).wait_recv()
-
-                @pl.when(forwards(m, t))
+                through_arrival(side, t, b).wait_recv()
+
+                @pl.when(passes_on(m, t))
                 def _():
-                    ring_copy(side, t, b).start()
+                    through_copy(side, t, b).start()
 
                 @pl.when((m < HALF) & (t == HALF - 1))
                 def _():
                     core_copy(b).start()
 
+            late = far - HALF * chunks
+            is_late = (m > HALF) & (m < NZ - 1) & (late >= 0) & (late < chunks)
+            is_early = (m == NZ - 2) & (near >= 0) & (near < chunks)
+
+            @pl.when(is_late | is_early)
+            def _():
+                e = jnp.where(is_late & (m == NZ - 2), 1, 0)
+                b = jnp.where(is_late, late, near)
+                extra_arrival(side, e, b).wait_recv()
+                extra_copy(side, e, b).start()
+
+            @pl.when((m == HALF) & (late == 0))
+            def _():
+                for b in range(hop, chunks):
+                    own_extra_copy(side, b).start()
+
         return carry
 
-    lax.fori_loop(0, 2 * chunks, ring_step, 0)
-
-    for copy in meta_in:
-        copy.wait_recv()
-    row_masks = jnp.concatenate([meta_ref[u, b, 4:5, :] for u in range(NZ) for b in range(per_device)], axis=0)
-    col_masks = jnp.concatenate(
-        [meta_ref[NZ + u, b, 5:6, :] for u in range(nx) for b in range(per_device)], axis=0
-    )
-    list_ref[...] = pair_list(place, row_masks, col_masks)
-
+    slots = (HALF + 1) * hop + HALF * chunks
     fars = far_axes_ref.shape[0]
     first_far = NZ + nx
-    steps = (NZ - 2) * chunks
-    each = -(-fars // steps)
-    axis = lax.broadcasted_iota(jnp.int32, (8, 3 * 128), 0)
-    wanted = lax.broadcasted_iota(jnp.int32, (8, 3 * 128), 1) // 128
-    spread = jnp.where(axis == wanted, 1.0, 0.0).astype(jnp.bfloat16)
+    each = -(-fars // (slots - MET_AT - 1))
+    at_end = (z == 0) | (z == NZ - 1)
+    listed_at = jnp.where(at_end, LISTED_AT[0], LISTED_AT[1])
+    axis = lax.broadcasted_iota(jnp.int32, (4 * per_device, 3 * 128), 0)
+    wanted = lax.broadcasted_iota(jnp.int32, (4 * per_device, 3 * 128), 1) // 128 * per_device
 
     def spread_far(j):
-        tile = meta_ref[first_far + j // per_device, j % per_device].astype(jnp.bfloat16)
+        spread = jnp.where(axis == wanted + j % per_device, 1.0, 0.0).astype(jnp.bfloat16)
         far_axes_ref[j] = lax.dot_general(
-            tile, spread, (((0,), (0,)), ((), ())), preferred_element_type=F32
+            meta_ref[first_far + j // per_device], spread, (((0,), (0,)), ((), ())), preferred_element_type=F32
         )
 
-    def ring_step_and_far(s, carry):
+    def list_pairs():
+        masks = [meta_ref[u].astype(F32)[3 * per_device :] for u in range(NZ + nx)]
+        row_masks = jnp.concatenate(masks[:NZ], axis=0)
+        col_masks = jnp.concatenate(masks[NZ:], axis=0)
+        list_ref[...] = pair_list(place, row_masks, col_masks)
+        for u in range(NZ + nx):
+            tile = meta_ref[u].astype(F32)
+            for b in range(per_device):
+                for c in range(3):
+                    row = c * per_device + b
+                    own_axes_ref[u * per_device + b, c : c + 1, :] = tile[row : row + 1]
+
+    def ring_and_more(s, carry):
         ring_step(s, carry)
+
+        @pl.when(s == MET_AT)
+        def _():
+            for copy in meta_in:
+                copy.wait_recv()
+
+        @pl.when(s == listed_at)
+        def _():
+            list_pairs()
+
         for e in range(each):
-            j = (s - 2 * chunks) * each + e
-
-            @pl.when(j < fars)
+            j = (s - MET_AT - 1) * each + e
+
+            @pl.when((j >= 0) & (j < fars))
             def _():
                 spread_far(j)
 
         return carry
 
-    lax.fori_loop(2 * chunks, NZ * chunks, ring_step_and_far, 0)
+    lax.fori_loop(hop, slots, ring_and_more, 0)
+
+    for side in (0, 1):
+
+        @pl.when(mirrored(side) == NZ - 1)
+        def _():
+            def kept(s, carry):
+                extra_arrival(side, s // chunks, s % chunks).wait_recv()
+                return carry
+
+            lax.fori_loop(0, (HALF - 1) * chunks, kept, 0)
+
 
     for copy in y_in + x_in:
         copy.wait_recv()
@@ -397,31 +445,40 @@
         copy.wait()
     for copy in y_out + x_out + meta_out + [core_own]:
         copy.wait_send()
-    for b in range(chunks):
+    def sent(b, carry):
         core_copy(b).wait_send()
         for side in (0, 1):
-
-            @pl.when(mirrored(side) < NZ - 1)
+            m = mirrored(side)
+
+            @pl.when(m < HALF)
             def _():
                 own_copy(side, b).wait_send()
 
-    def sent_step(s, carry):
-        t, b = s // chunks, s % chunks
-        for side in (0, 1):
-
-            @pl.when(forwards(mirrored(side), t))
-            def _():
-                ring_copy(side, t, b).wait_send()
+            @pl.when(sends_extra(m))
+            def _():
+                own_extra_copy(side, b).wait_send()
+
+            for t in range(HALF):
+
+                @pl.when(passes_on(m, t))
+                def _():
+                    through_copy(side, t, b).wait_send()
+
+            for e in range(2):
+
+                @pl.when((m > HALF + e) & (m < NZ - 1))
+                def _():
+                    extra_copy(side, e, b).wait_send()
 
         return carry
 
-    lax.fori_loop(0, (NZ - 1) * chunks, sent_step, 0)
-
-
-UNROLL = 4
-
-
-def pair_kernel(rows, own, shift, list_ref, blocks, meta_ref, far_axes, out_ref, acc):
+    lax.fori_loop(0, chunks, sent, 0)
+
+
+UNROLL = 8
+
+
+def pair_kernel(rows, own, shift, list_ref, blocks, own_axes_ref, far_axes, out_ref, acc):
     per_device = out_ref.shape[1] // 4
     acc[...] = jnp.zeros_like(acc)
     count = list_ref[MAX_PAIRS_ROWS, 0]
@@ -433,7 +490,7 @@
         weights = lax.dot_general(
             blocks[far_block], blocks[own_block], (((1,), (1,)), ((), ())), preferred_element_type=F32
         )
-        tile = meta_ref[acc_slot]
+        tile = own_axes_ref[acc_slot]
         own_axes = [jnp.broadcast_to(tile[c : c + 1], (8, 128)) for c in range(3)]
         sums = [jnp.zeros((8, 128), F32) for _ in range(3)]
         for r in range(16):
@@ -521,12 +578,12 @@
     fars = (ny + 4) * per_device
     small = pltpu.CompilerParams(vmem_limit_bytes=8 * 1024 * 1024)
     vmem = pl.BlockSpec(memory_space=pltpu.VMEM)
-    blocks, meta, far_axes, listing = pl.pallas_call(
+    blocks, own_axes, far_axes, listing = pl.pallas_call(
         functools.partial(gather_kernel, nx, ny),
         name="gather",
         out_shape=(
             jax.ShapeDtypeStruct((units, per_device, size_block, conditions), jnp.bfloat16),
-            jax.ShapeDtypeStruct((metas, per_device, 8, 128), F32),
+            jax.ShapeDtypeStruct(((NZ + nx) * per_device, 8, 128), F32),
             jax.ShapeDtypeStruct((fars, size_block, 3 * 128), F32),
             jax.ShapeDtypeStruct((8, 128), jnp.int32),
         ),
@@ -538,9 +595,12 @@
             pltpu.VMEM((1, per_device), jnp.int32),
             pltpu.VMEM((per_device, near_cols.shape[2]), jnp.int32),
             pltpu.VMEM((1, per_device), jnp.int32),
-            pltpu.VMEM((per_device, 8, 128), F32),
-            dma((2, NZ, per_device * SPLIT)),
-            dma((2, NZ, per_device * SPLIT)),
+            pltpu.VMEM((2, 4 * per_device, 128), jnp.bfloat16),
+            pltpu.VMEM((metas, 4 * per_device, 128), jnp.bfloat16),
+            dma((2, HALF + 1, per_device * SPLIT)),
+            dma((2, HALF, per_device * SPLIT)),
+            dma((2, HALF, per_device * SPLIT)),
+            dma((2, HALF, per_device * SPLIT)),
             dma((per_device * SPLIT + 1,)),
             dma((per_device * SPLIT + 1,)),
             dma((max(ny - 1, 1),)),
@@ -583,7 +643,7 @@
     )(
         listing,
         blocks.reshape(units * per_device, size_block, conditions),
-        meta.reshape(metas * per_device, 8, 128),
+        own_axes,
         far_axes,
     )
     total = pl.pallas_call(

time: 87.1 us -> 77.5 us (0.89)
  Pallas kernels: 85.8 us -> 76.5 us
    pallas_call x1, Pallas kernels: 68.3 us -> 61.3 us  [shards(): pl.pallas_call(functools.partial(gather_kernel, nx, ny), name='gather', o...]
    pallas_call x1, Pallas kernels: 12.6 us -> 10.3 us  [shards(): pl.pallas_call(functools.partial(return_kernel, nx, ny), name='sums', out...]
where the time goes in v3:
time: 77.5 us; the launch traced here: 77.2 us
  Pallas kernels  76.5 us (99%)
    pallas_call x1, Pallas kernels, shards(): pl.pallas_call(functools.partial(gather_kernel, nx, ny), name='gather', o...  61.3 us
    pallas_call x1, Pallas kernels, shards(): pl.pallas_call(functools.partial(return_kernel, nx, ny), name='sums', out...  10.3 us
    pallas_call x1, Pallas kernels, shards(): pl.pallas_call(functools.partial(pair_kernel, rows, own, shift), name='pa...  4.97 us

profile of v3, /device:TPU:1, one launch (start us, length us, event | category | flops | bytes accessed | tf_op | source)
XLA Modules:
  0.0 77.2 jit_solution(3858660990250903278)
XLA Ops:
  0.0 61.3 %gather.1 = (bf16[22,4,128,256]{3,2,1,0:T(8,128)(2,1)S(1)}, f32[48,8,128]{2,1,0:T(8,128)S(1)}, f32[32,128,384]{2,1,0:T(8,128)S(1)}, s32[8,128]{1,0:T(8,128)S(1)}) custom-call(bf16[4,128,256]{2,1,0:T(8,128)(2,1)} %bitcast.13, bf16[4,128,256]{2,1,0:T(8,128)(2,1)} %bitcast.14, bf16[3,4,128]{2,1,0:T(4,128)(2,1)} %bitcast.15, s32[4,32]{1,0:T(4,128)} %bitcast.16, ...), custom_call_target="tpu_custom_call" | custom-call | tf_op jit(solution)/shard_map/gather/pallas_call | solution.py:581
  61.3 5.0 %pairs.1.parts_ref = f32[12,16,128]{2,1,0:T(8,128)S(1)} custom-call(s32[8,128]{1,0:T(8,128)S(1)} %get-tuple-element.9.list_ref, bf16[88,128,256]{2,1,0:T(8,128)(2,1)S(1)} %bitcast.11, f32[48,8,128]{2,1,0:T(8,128)S(1)} %get-tuple-element.11.own_axes_ref, f32[32,128,384]{2,1,0:T(8,128)S(1)} %get-tuple-element.12.far_axes), custom_call_target="tpu_custom_call" | custom-call | tf_op jit(solution)/shard_map/pairs/pallas_call | solution.py:635
  66.3 10.3 %sums.1 = f32[3,4,128]{2,1,0:T(4,128)S(1)} custom-call(f32[12,16,128]{2,1,0:T(8,128)S(1)} %pairs.1.parts_ref), custom_call_target="tpu_custom_call" | custom-call | tf_op jit(solution)/shard_map/sums/pallas_call | solution.py:649
  76.6 0.6 copy.9

commit v4 on v3

--- a/solution.py
+++ b/solution.py
@@ -16,6 +16,7 @@
 AHEAD = NZ
 SIBLING = AHEAD + HALF
 SOURCES_Y = SIBLING + 2
+COLS_AT = 4
 MAX_PAIRS_ROWS = 6
 SPLIT = 1
 MET_AT = 8
@@ -97,9 +98,12 @@
     live = jnp.concatenate([dot(row_mask.astype(bf), pick_row), dot(col_mask.astype(bf), pick_col)], axis=0)
     before = dot(live.astype(bf), jnp.where(lane < k, 1.0, 0.0).astype(bf))
     totals = jnp.broadcast_to(jnp.sum(live, axis=1, keepdims=True), (own, 128))
-    above = lax.broadcasted_iota(jnp.int32, (own, own), 0) > lax.broadcasted_iota(jnp.int32, (own, own), 1)
+    one = lax.broadcasted_iota(jnp.int32, (own, own), 0)
+    other = lax.broadcasted_iota(jnp.int32, (own, own), 1)
+    above = (one > other) & ((one < rows) | (other >= rows))
     offset = dot(jnp.where(above, 1.0, 0.0).astype(bf), totals.astype(bf))
-    rank = jnp.where(live > 0.5, before + offset, -1.0)
+    first = jnp.where(lax.broadcasted_iota(jnp.int32, (own, 128), 0) < rows, 0.0, 128.0 * COLS_AT)
+    rank = jnp.where(live > 0.5, before + offset + first, -1.0)
 
     a = lax.broadcasted_iota(jnp.int32, (own, 128), 0)
     k = lax.broadcasted_iota(jnp.int32, (own, 128), 1)
@@ -124,8 +128,8 @@
         for r in range(MAX_PAIRS_ROWS):
             packed[r] = packed[r] + jnp.where(rank_one == slots + 128.0 * r, code_one, 0.0)
     listing = [jnp.sum(part, axis=0, keepdims=True) for part in packed]
-    count = jnp.broadcast_to(jnp.sum(jnp.sum(live, axis=1, keepdims=True), axis=0, keepdims=True), (2, 128))
-    return jnp.concatenate(listing + [count], axis=0).astype(jnp.int32)
+    counts = [jnp.sum(part, axis=0, keepdims=True) for part in (totals[:rows], totals[rows:])]
+    return jnp.concatenate(listing + counts, axis=0).astype(jnp.int32)
 
 
 def gather_kernel(
@@ -476,55 +480,115 @@
 
 
 UNROLL = 8
+STATIC_ROWS = 64
+STATIC_COLS = 40
+
+
+def decode(code, rows, shift):
+    own_block = code & 127
+    return own_block, (code >> 7) & 127, code >> 14, jnp.where(own_block < rows, own_block, own_block - shift)
+
+
+def pair_term(blocks, own_axes_ref, far_axes, entry):
+    own_block, far_block, far_slot, acc_slot = entry
+    weights = lax.dot_general(
+        blocks[far_block], blocks[own_block], (((1,), (1,)), ((), ())), preferred_element_type=F32
+    )
+    tile = own_axes_ref[acc_slot]
+    own_axes = [jnp.broadcast_to(tile[c : c + 1], (8, 128)) for c in range(3)]
+    sums = [jnp.zeros((8, 128), F32) for _ in range(3)]
+    for r in range(16):
+        at = slice(8 * r, 8 * r + 8)
+        d = [far_axes[far_slot, at, 128 * c : 128 * c + 128] - own_axes[c] for c in range(3)]
+        inverse = lax.rsqrt(d[0] * d[0] + d[1] * d[1] + d[2] * d[2] + EPS2)
+        scaled = weights[at] * (inverse * inverse * inverse)
+        sums = [sums[c] + d[c] * scaled for c in range(3)]
+    return sums
 
 
 def pair_kernel(rows, own, shift, list_ref, blocks, own_axes_ref, far_axes, out_ref, acc):
     per_device = out_ref.shape[1] // 4
-    acc[...] = jnp.zeros_like(acc)
-    count = list_ref[MAX_PAIRS_ROWS, 0]
-
-    def one_pair(k):
-        code = list_ref[k // 128, k % 128]
-        own_block, far_block, far_slot = code & 127, (code >> 7) & 127, code >> 14
-        acc_slot = jnp.where(own_block < rows, own_block, own_block - shift)
-        weights = lax.dot_general(
-            blocks[far_block], blocks[own_block], (((1,), (1,)), ((), ())), preferred_element_type=F32
-        )
-        tile = own_axes_ref[acc_slot]
-        own_axes = [jnp.broadcast_to(tile[c : c + 1], (8, 128)) for c in range(3)]
-        sums = [jnp.zeros((8, 128), F32) for _ in range(3)]
-        for r in range(16):
-            at = slice(8 * r, 8 * r + 8)
-            d = [far_axes[far_slot, at, 128 * c : 128 * c + 128] - own_axes[c] for c in range(3)]
-            inverse = lax.rsqrt(d[0] * d[0] + d[1] * d[1] + d[2] * d[2] + EPS2)
-            scaled = weights[at] * (inverse * inverse * inverse)
-            sums = [sums[c] + d[c] * scaled for c in range(3)]
-        return jnp.where(k < count, acc_slot, own), sums
-
-    def step(i, carry):
-        done = [one_pair(i * UNROLL + u) for u in range(UNROLL)]
-        for slot, sums in done:
+    out_ref[...] = jnp.zeros_like(out_ref)
+    kinds = []
+    for kind, (first, done) in enumerate(((0, STATIC_ROWS), (COLS_AT, STATIC_COLS))):
+        kinds.append((first, done, list_ref[MAX_PAIRS_ROWS + kind, 0]))
+
+    @pl.when((kinds[0][2] > STATIC_ROWS) | (kinds[1][2] > STATIC_COLS))
+    def _():
+        acc[...] = jnp.zeros_like(acc)
+        for first, done, count in kinds:
+
+            def step(i, carry):
+                for u in range(UNROLL):
+                    k = i * UNROLL + u
+                    entry = decode(list_ref[first + k // 128, k % 128], rows, shift)
+                    sums = pair_term(blocks, own_axes_ref, far_axes, entry)
+                    slot = jnp.where(k < count, entry[3], own)
+                    for c in range(3):
+                        acc[slot, c] = acc[slot, c] + sums[c]
+                return carry
+
+            lax.fori_loop(done // UNROLL, (count + UNROLL - 1) // UNROLL, step, 0)
+        for a in range(own):
             for c in range(3):
-                acc[slot, c] = acc[slot, c] + sums[c]
-        return carry
-
-    lax.fori_loop(0, (count + UNROLL - 1) // UNROLL, step, 0)
-    out_ref[...] = jnp.zeros_like(out_ref)
-    for a in range(own):
-        for c in range(3):
-            row = c * per_device + a % per_device
-            out_ref[a // per_device, row : row + 1, :] = jnp.sum(acc[a, c], axis=0, keepdims=True)
-
-
-def return_kernel(nx, ny, parts_ref, out_ref, landed, send_sem, recv_sem):
+                row = c * per_device + a % per_device
+                out_ref[a // per_device, row : row + 1, :] = jnp.sum(acc[a, c], axis=0, keepdims=True)
+
+
+def sums_kernel(
+    nx,
+    ny,
+    rows,
+    own,
+    shift,
+    list_ref,
+    listing_ref,
+    blocks,
+    own_axes_ref,
+    far_axes,
+    rest_ref,
+    out_ref,
+    terms,
+    parts_ref,
+    landed,
+    send_sem,
+    recv_sem,
+):
     place = Place(nx, ny)
     z, x = place.z, place.x
     others_z, others_x = place.others_z(), place.others_x()
     met = [device for _, device in others_z] + [device for _, device in others_x]
     greet(met)
-    landed[z] = parts_ref[z]
-    landed[NZ + x] = parts_ref[NZ + x]
-    await_greetings(len(met))
+    per_device = out_ref.shape[1]
+
+    terms[...] = jnp.zeros_like(terms)
+    k = lax.broadcasted_iota(jnp.int32, (own, 128), 1)
+    owner = lax.broadcasted_iota(jnp.int32, (own, 128), 0)
+
+    def static_pairs(kind, first, length, units):
+        def step(i, carry):
+            done = []
+            for u in range(UNROLL):
+                entry = decode(list_ref[first, i * UNROLL + u], rows, shift)
+                sums = pair_term(blocks, own_axes_ref, far_axes, entry)
+                done.append(jnp.concatenate([jnp.sum(part, axis=0, keepdims=True) for part in sums], axis=1))
+            terms[pl.ds(pl.multiple_of(i * UNROLL, UNROLL), UNROLL), :] = jnp.concatenate(done, axis=0)
+            return carry
+
+        lax.fori_loop(0, length // UNROLL, step, 0)
+        codes = jnp.broadcast_to(listing_ref[first : first + 1, :], (own, 128))
+        at = MAX_PAIRS_ROWS + kind
+        count = jnp.broadcast_to(listing_ref[at : at + 1, :], (own, 128))
+        mine = (decode(codes, rows, shift)[3] == owner) & (k < count) & (k < length)
+        owns = jnp.where(mine, 1.0, 0.0)
+        acc = jnp.dot(owns, terms[...], preferred_element_type=F32, precision=lax.Precision.HIGHEST)
+        for u in units:
+            for c in range(3):
+                at = slice(c * per_device, (c + 1) * per_device)
+                parts_ref[u, at, :] = (
+                    rest_ref[u, at, :] + acc[u * per_device : (u + 1) * per_device, 128 * c : 128 * c + 128]
+                )
+
     outgoing, incoming = [], []
 
     def both(s, theirs, mine, source, device):
@@ -544,14 +608,21 @@
         both(d, other, z, (z + NZ - 1 - d) % NZ, device)
     for d, (other, device) in enumerate(others_x):
         both(NZ + d, NZ + other, NZ + x, NZ + (x + nx - 1 - d) % nx, device)
-    for copy in outgoing:
+
+    static_pairs(0, 0, STATIC_ROWS, range(NZ))
+    await_greetings(len(met))
+    for copy in outgoing[: NZ - 1]:
         copy.start()
+    static_pairs(1, COLS_AT, STATIC_COLS, range(NZ, NZ + nx))
+    for copy in outgoing[NZ - 1 :]:
+        copy.start()
+    landed[z] = parts_ref[z]
+    landed[NZ + x] = parts_ref[NZ + x]
     for copy in incoming:
         copy.wait_recv()
     total = landed[0]
     for u in range(1, NZ + nx):
         total = total + landed[u]
-    per_device = out_ref.shape[1]
     for c in range(3):
         out_ref[c] = total[c * per_device : (c + 1) * per_device]
     for copy in outgoing:
@@ -632,35 +703,35 @@
     rows = NZ * per_device
     own = rows + nx * per_device
     shift = (SOURCES_Y + ny) * per_device - rows
-    parts = pl.pallas_call(
+    blocks = blocks.reshape(units * per_device, size_block, conditions)
+    smem = pl.BlockSpec(memory_space=pltpu.SMEM)
+    parts_shape = (NZ + nx, 4 * per_device, 128)
+    rest = pl.pallas_call(
         functools.partial(pair_kernel, rows, own, shift),
         name="pairs",
-        out_shape=jax.ShapeDtypeStruct((NZ + nx, 4 * per_device, 128), F32),
-        in_specs=[pl.BlockSpec(memory_space=pltpu.SMEM), vmem, vmem, vmem],
+        out_shape=jax.ShapeDtypeStruct(parts_shape, F32),
+        in_specs=[smem, vmem, vmem, vmem],
         out_specs=vmem,
         scratch_shapes=[pltpu.VMEM((own + 1, 3, 8, 128), F32)],
         compiler_params=small,
-    )(
-        listing,
-        blocks.reshape(units * per_device, size_block, conditions),
-        own_axes,
-        far_axes,
-    )
+    )(listing, blocks, own_axes, far_axes)
     total = pl.pallas_call(
-        functools.partial(return_kernel, nx, ny),
+        functools.partial(sums_kernel, nx, ny, rows, own, shift),
         name="sums",
         out_shape=jax.ShapeDtypeStruct((3, per_device, 128), F32),
-        in_specs=[vmem],
+        in_specs=[smem] + [vmem] * 5,
         out_specs=vmem,
         scratch_shapes=[
-            pltpu.VMEM((NZ + nx, 4 * per_device, 128), F32),
+            pltpu.VMEM((128, 3 * 128), F32),
+            pltpu.VMEM(parts_shape, F32),
+            pltpu.VMEM(parts_shape, F32),
             dma((NZ + nx,)),
             dma((NZ + nx,)),
         ],
         compiler_params=pltpu.CompilerParams(
             collective_id=1, has_side_effects=True, vmem_limit_bytes=8 * 1024 * 1024
         ),
-    )(parts)
+    )(listing, listing, blocks, own_axes, far_axes, rest)
     return jnp.transpose(total, (1, 0, 2))[None]
 
 

time: 77.5 us -> 75.3 us (0.972)
  Pallas kernels: 76.5 us -> 74.6 us
    pallas_call x1, Pallas kernels: 4.97 us -> 0.61 us  [shards(): pl.pallas_call(functools.partial(pair_kernel, rows, own, shift), name='pa...]
    pallas_call x1, Pallas kernels: 10.3 us -> 12.6 us  [shards(): pl.pallas_call(functools.partial(sums_kernel, nx, ny, rows, own, shift),...]
where the time goes in v4:
time: 75.3 us; the launch traced here: 75.2 us
  Pallas kernels  74.6 us (99%)
    pallas_call x1, Pallas kernels, shards(): pl.pallas_call(functools.partial(gather_kernel, nx, ny), name='gather', o...  61.3 us
    pallas_call x1, Pallas kernels, shards(): pl.pallas_call(functools.partial(sums_kernel, nx, ny, rows, own, shift),...  12.6 us

profile of v4, /device:TPU:1, one launch (start us, length us, event | category | flops | bytes accessed | tf_op | source)
XLA Modules:
  0.0 75.2 jit_solution(8407859507557689945)
XLA Ops:
  0.0 61.3 %gather.1 = (bf16[22,4,128,256]{3,2,1,0:T(8,128)(2,1)S(1)}, f32[48,8,128]{2,1,0:T(8,128)S(1)}, f32[32,128,384]{2,1,0:T(8,128)S(1)}, s32[8,128]{1,0:T(8,128)S(1)}) custom-call(bf16[4,128,256]{2,1,0:T(8,128)(2,1)} %bitcast.14, bf16[4,128,256]{2,1,0:T(8,128)(2,1)} %bitcast.15, bf16[3,4,128]{2,1,0:T(4,128)(2,1)} %bitcast.16, s32[4,32]{1,0:T(4,128)} %bitcast.17, ...), custom_call_target="tpu_custom_call" | custom-call | tf_op jit(solution)/shard_map/gather/pallas_call | solution.py:652
  61.3 0.6 pairs.1.rest_ref
  61.9 12.6 %sums.1 = f32[3,4,128]{2,1,0:T(4,128)S(1)} custom-call(s32[8,128]{1,0:T(8,128)S(1)} %get-tuple-element.9.list_ref.listing_ref, s32[8,128]{1,0:T(8,128)S(1)} %get-tuple-element.9.list_ref.listing_ref, bf16[88,128,256]{2,1,0:T(8,128)(2,1)S(1)} %bitcast.12, f32[48,8,128]{2,1,0:T(8,128)S(1)} %get-tuple-element.11.own_axes_ref, ...), custom_call_target="tpu_custom_call" | custom-call | tf_op jit(solution)/shard_map/sums/pallas_call | solution.py:718
  74.6 0.6 copy.9

commit v5 on v4

--- a/solution.py
+++ b/solution.py
@@ -14,8 +14,7 @@
 NZ = 8
 HALF = NZ // 2
 AHEAD = NZ
-SIBLING = AHEAD + HALF
-SOURCES_Y = SIBLING + 2
+SOURCES_Y = AHEAD + HALF
 COLS_AT = 4
 MAX_PAIRS_ROWS = 6
 SPLIT = 1
@@ -51,11 +50,16 @@
     def others_y(self):
         return [self.at(y=(self.y + d) % self.ny) for d in range(1, self.ny)]
 
-    def others_x(self):
-        return [((self.x + d) % self.nx, self.at(x=(self.x + d) % self.nx)) for d in range(1, self.nx)]
-
-    def others_hc(self):
-        return [self.at(h=(self.h + rel // 2) % 2, c=(self.c + rel % 2) % 2) for rel in (1, 2, 3)]
+    def others_xc(self):
+        found = []
+        for d in range(1, 2 * self.nx):
+            to_x, from_x = (self.x + d // 2) % self.nx, (self.x + self.nx - d // 2) % self.nx
+            c = (self.c + d % 2) % 2
+            found.append((to_x * 2 + c, from_x * 2 + c, self.at(x=to_x, c=c)))
+        return found
+
+    def opposite(self):
+        return self.at(h=1 - self.h)
 
 
 def greet(devices):
@@ -88,12 +92,11 @@
     own = rows + cols
     lane = lax.broadcasted_iota(jnp.int32, (128, 128), 0)
     k = lax.broadcasted_iota(jnp.int32, (128, 128), 1)
-    rel = k // 4
     from_row = (k // 4) * (NZ * 4) + z * 4 + k % 4
-    from_col = x * 16 + ((rel // 2 + h) % 2) * 8 + ((rel + c) % 2) * 4 + k % 4
+    from_col = x * 16 + (k // 4 + h) % 2 * 8 + c * 4 + k % 4
     bf = jnp.bfloat16
     pick_row = jnp.where((lane == from_row) & (k < ny * 4), 1.0, 0.0).astype(bf)
-    pick_col = jnp.where((lane == from_col) & (k < 16), 1.0, 0.0).astype(bf)
+    pick_col = jnp.where((lane == from_col) & (k < 8), 1.0, 0.0).astype(bf)
     dot = functools.partial(jnp.dot, preferred_element_type=F32)
     live = jnp.concatenate([dot(row_mask.astype(bf), pick_row), dot(col_mask.astype(bf), pick_col)], axis=0)
     before = dot(live.astype(bf), jnp.where(lane < k, 1.0, 0.0).astype(bf))
@@ -107,10 +110,7 @@
 
     a = lax.broadcasted_iota(jnp.int32, (own, 128), 0)
     k = lax.broadcasted_iota(jnp.int32, (own, 128), 1)
-    rel = k // 4
-    unit = jnp.where(
-        rel == 0, z, jnp.where(rel == 1, SIBLING, jnp.where(rel == 2, AHEAD + z % HALF, SIBLING + 1))
-    )
+    unit = jnp.where(k // 4 == 0, z, AHEAD + z % HALF)
     is_row = a < rows
     own_block = jnp.where(is_row, a, a - rows + sources_x * 4)
     far_block = jnp.where(is_row, SOURCES_Y * 4 + k, unit * 4 + k % 4)
@@ -157,8 +157,6 @@
     through_recv,
     extra_send,
     extra_recv,
-    core_send,
-    core_recv,
     y_send,
     y_recv,
     x_send,
@@ -188,15 +186,10 @@
     sources_x = SOURCES_Y + ny
     right, left = place.beside(True), place.beside(False)
     sides = (right, left)
-    others_z, others_y, others_x, others_hc = (
-        place.others_z(),
-        place.others_y(),
-        place.others_x(),
-        place.others_hc(),
-    )
-    sibling = others_hc[0]
-    met = [device for _, device in others_z] + others_y + [device for _, device in others_x] + others_hc
-    met = met + [right, left]
+    others_z, others_y, others_xc = place.others_z(), place.others_y(), place.others_xc()
+    opposite = place.opposite()
+    met = [device for _, device in others_z] + others_y + [device for _, _, device in others_xc]
+    met = met + [opposite, right, left]
     greet(met)
 
     for copy in smalls:
@@ -243,69 +236,45 @@
         return remote(
             part(blocks_ref.at[unit], b),
             part(blocks_ref.at[jnp.where(m == NZ - 1, crossed, unit)], b),
-            through_send.at[side, t + 1, b],
+            through_send.at[side, t + 1],
             through_recv.at[side, jnp.where(m < HALF, t + 1, t), b],
             sides[side],
         )
 
     def through_arrival(side, t, b):
         slot = part(blocks_ref.at[through_unit(side, mirrored(side), t)], b)
-        return remote(slot, slot, through_send.at[side, t + 1, b], through_recv.at[side, t, b], sides[side])
+        return remote(slot, slot, through_send.at[side, t + 1], through_recv.at[side, t, b], sides[side])
 
     def extra_copy(side, e, b):
         slot = part(blocks_ref.at[slot_of(side, mirrored(side) - 1 - e)], b)
-        return remote(slot, slot, extra_send.at[side, e + 1, b], extra_recv.at[side, e + 1, b], sides[side])
+        return remote(slot, slot, extra_send.at[side, e + 1], extra_recv.at[side, e + 1, b], sides[side])
 
     def extra_arrival(side, e, b):
         slot = part(blocks_ref.at[slot_of(side, mirrored(side) - 1 - e)], b)
-        return remote(slot, slot, extra_send.at[side, e + 1, b], extra_recv.at[side, e, b], sides[side])
+        return remote(slot, slot, extra_send.at[side, e + 1], extra_recv.at[side, e, b], sides[side])
 
     def own_copy(side, b):
-        send, recv = through_send.at[side, 0, b], through_recv.at[side, 0, b]
+        send, recv = through_send.at[side, 0], through_recv.at[side, 0, b]
         return remote(part(adjoint_ref, b), part(blocks_ref.at[z], b), send, recv, sides[side])
 
     def own_extra_copy(side, b):
-        send, recv = extra_send.at[side, 0, b], extra_recv.at[side, 0, b]
+        send, recv = extra_send.at[side, 0], extra_recv.at[side, 0, b]
         return remote(part(adjoint_ref, b), part(blocks_ref.at[z], b), send, recv, sides[side])
 
     def sends_extra(m):
         return (m >= HALF) & (m < NZ - 1)
 
-    def core_copy(b):
-        return remote(
-            part(blocks_ref.at[AHEAD + z % HALF], b),
-            part(blocks_ref.at[SIBLING + 1], b),
-            core_send.at[b],
-            core_recv.at[b],
-            sibling,
-        )
-
-    core_own = remote(
-        adjoint_ref, blocks_ref.at[SIBLING], core_send.at[chunks], core_recv.at[chunks], sibling
-    )
-
-    for b in range(chunks):
-        for side in (0, 1):
-            m = mirrored(side)
-
-            @pl.when(m < HALF)
-            def _():
-                own_copy(side, b).start()
-
-            @pl.when(sends_extra(m) & ((m > HALF) | (b < hop)))
-            def _():
-                own_extra_copy(side, b).start()
-
     metas = []
-    own_slots = [z, NZ + x, NZ + nx + y, NZ + nx + ny]
+    mine = x * 2 + place.c
+    first_y = NZ + 2 * nx
+    own_slots = [z, NZ + mine, first_y + y, first_y + ny]
     for d, (_, device) in enumerate(others_z):
         metas.append((0, own_slots[0], d, device, (z + NZ - 1 - d) % NZ))
-    for d, (_, device) in enumerate(others_x):
-        metas.append((1, own_slots[1], NZ + d, device, NZ + (x + nx - 1 - d) % nx))
+    for d, (_, source, device) in enumerate(others_xc):
+        metas.append((1, own_slots[1], NZ + d, device, NZ + source))
     for d, device in enumerate(others_y):
-        metas.append((1, own_slots[2], NZ + nx + d, device, NZ + nx + (y + ny - 1 - d) % ny))
-    for d, device in enumerate(others_hc):
-        metas.append((1, NZ + nx + ny + 1 + d, NZ + nx + ny + d, device, NZ + nx + ny + 1 + d))
+        metas.append((1, own_slots[2], first_y + d, device, first_y + (y + ny - 1 - d) % ny))
+    metas.append((1, first_y + ny + 1, first_y + ny, opposite, first_y + ny + 1))
     meta_out = [
         remote(own_meta.at[which], meta_ref.at[slot], meta_send.at[s], meta_recv.at[s], device)
         for which, slot, s, device, _ in metas
@@ -316,22 +285,33 @@
     ]
     for copy in meta_out:
         copy.start()
-    core_own.start()
+    for b in range(chunks):
+        for side in (0, 1):
+            m = mirrored(side)
+
+            @pl.when(m < HALF)
+            def _():
+                own_copy(side, b).start()
+
+            @pl.when(sends_extra(m) & ((m > HALF) | (b < hop)))
+            def _():
+                own_extra_copy(side, b).start()
+
     y_out, y_in, x_out, x_in = [], [], [], []
     for d, device in enumerate(others_y):
         sems = (y_send.at[d], y_recv.at[d], device)
         y_out.append(remote(source_ref, blocks_ref.at[SOURCES_Y + y], *sems))
         y_in.append(remote(source_ref, blocks_ref.at[SOURCES_Y + (y + ny - 1 - d) % ny], *sems))
-    for d, (_, device) in enumerate(others_x):
+    for d, (_, source, device) in enumerate(others_xc):
         sems = (x_send.at[d], x_recv.at[d], device)
-        x_out.append(remote(source_ref, blocks_ref.at[sources_x + x], *sems))
-        x_in.append(remote(source_ref, blocks_ref.at[sources_x + (x + nx - 1 - d) % nx], *sems))
+        x_out.append(remote(source_ref, blocks_ref.at[sources_x + mine], *sems))
+        x_in.append(remote(source_ref, blocks_ref.at[sources_x + source], *sems))
     for copy in y_out + x_out:
         copy.start()
     locals_ = [
         pltpu.make_async_copy(adjoint_ref, blocks_ref.at[z], local_sem.at[0]),
         pltpu.make_async_copy(source_ref, blocks_ref.at[SOURCES_Y + y], local_sem.at[1]),
-        pltpu.make_async_copy(source_ref, blocks_ref.at[sources_x + x], local_sem.at[2]),
+        pltpu.make_async_copy(source_ref, blocks_ref.at[sources_x + mine], local_sem.at[2]),
     ]
     for copy in locals_:
         copy.start()
@@ -357,10 +337,6 @@
                 def _():
                     through_copy(side, t, b).start()
 
-                @pl.when((m < HALF) & (t == HALF - 1))
-                def _():
-                    core_copy(b).start()
-
             late = far - HALF * chunks
             is_late = (m > HALF) & (m < NZ - 1) & (late >= 0) & (late < chunks)
             is_early = (m == NZ - 2) & (near >= 0) & (near < chunks)
@@ -381,7 +357,7 @@
 
     slots = (HALF + 1) * hop + HALF * chunks
     fars = far_axes_ref.shape[0]
-    first_far = NZ + nx
+    first_far = first_y
     each = -(-fars // (slots - MET_AT - 1))
     at_end = (z == 0) | (z == NZ - 1)
     listed_at = jnp.where(at_end, LISTED_AT[0], LISTED_AT[1])
@@ -395,11 +371,11 @@
         )
 
     def list_pairs():
-        masks = [meta_ref[u].astype(F32)[3 * per_device :] for u in range(NZ + nx)]
+        masks = [meta_ref[u].astype(F32)[3 * per_device :] for u in range(first_y)]
         row_masks = jnp.concatenate(masks[:NZ], axis=0)
         col_masks = jnp.concatenate(masks[NZ:], axis=0)
         list_ref[...] = pair_list(place, row_masks, col_masks)
-        for u in range(NZ + nx):
+        for u in range(first_y):
             tile = meta_ref[u].astype(F32)
             for b in range(per_device):
                 for c in range(3):
@@ -442,46 +418,40 @@
 
     for copy in y_in + x_in:
         copy.wait_recv()
-    for b in range(chunks):
-        core_copy(b).wait_recv()
-    core_own.wait_recv()
     for copy in locals_:
         copy.wait()
-    for copy in y_out + x_out + meta_out + [core_own]:
+    for copy in y_out + x_out + meta_out:
         copy.wait_send()
-    def sent(b, carry):
-        core_copy(b).wait_send()
-        for side in (0, 1):
-            m = mirrored(side)
-
-            @pl.when(m < HALF)
+    def unit_sent(semaphore):
+        remote(blocks_ref.at[z], blocks_ref.at[z], semaphore, through_recv.at[0, 0, 0], right).wait_send()
+
+    for side in (0, 1):
+        m = mirrored(side)
+
+        @pl.when(m < HALF)
+        def _():
+            unit_sent(through_send.at[side, 0])
+
+        @pl.when(sends_extra(m))
+        def _():
+            unit_sent(extra_send.at[side, 0])
+
+        for t in range(HALF):
+
+            @pl.when(passes_on(m, t))
             def _():
-                own_copy(side, b).wait_send()
-
-            @pl.when(sends_extra(m))
+                unit_sent(through_send.at[side, t + 1])
+
+        for e in range(2):
+
+            @pl.when((m > HALF + e) & (m < NZ - 1))
             def _():
-                own_extra_copy(side, b).wait_send()
-
-            for t in range(HALF):
-
-                @pl.when(passes_on(m, t))
-                def _():
-                    through_copy(side, t, b).wait_send()
-
-            for e in range(2):
-
-                @pl.when((m > HALF + e) & (m < NZ - 1))
-                def _():
-                    extra_copy(side, e, b).wait_send()
-
-        return carry
-
-    lax.fori_loop(0, chunks, sent, 0)
+                unit_sent(extra_send.at[side, e + 1])
 
 
 UNROLL = 8
 STATIC_ROWS = 64
-STATIC_COLS = 40
+STATIC_COLS = 24
 
 
 def decode(code, rows, shift):
@@ -556,8 +526,9 @@
 ):
     place = Place(nx, ny)
     z, x = place.z, place.x
-    others_z, others_x = place.others_z(), place.others_x()
-    met = [device for _, device in others_z] + [device for _, device in others_x]
+    others_z, others_xc = place.others_z(), place.others_xc()
+    mine = x * 2 + place.c
+    met = [device for _, device in others_z] + [device for _, _, device in others_xc]
     greet(met)
     per_device = out_ref.shape[1]
 
@@ -579,8 +550,8 @@
         codes = jnp.broadcast_to(listing_ref[first : first + 1, :], (own, 128))
         at = MAX_PAIRS_ROWS + kind
         count = jnp.broadcast_to(listing_ref[at : at + 1, :], (own, 128))
-        mine = (decode(codes, rows, shift)[3] == owner) & (k < count) & (k < length)
-        owns = jnp.where(mine, 1.0, 0.0)
+        has = (decode(codes, rows, shift)[3] == owner) & (k < count) & (k < length)
+        owns = jnp.where(has, 1.0, 0.0)
         acc = jnp.dot(owns, terms[...], preferred_element_type=F32, precision=lax.Precision.HIGHEST)
         for u in units:
             for c in range(3):
@@ -606,22 +577,22 @@
 
     for d, (other, device) in enumerate(others_z):
         both(d, other, z, (z + NZ - 1 - d) % NZ, device)
-    for d, (other, device) in enumerate(others_x):
-        both(NZ + d, NZ + other, NZ + x, NZ + (x + nx - 1 - d) % nx, device)
+    for d, (other, source, device) in enumerate(others_xc):
+        both(NZ + d, NZ + other, NZ + mine, NZ + source, device)
 
     static_pairs(0, 0, STATIC_ROWS, range(NZ))
     await_greetings(len(met))
-    for copy in outgoing[: NZ - 1]:
+    for copy in outgoing[: NZ - 1][::-1]:
         copy.start()
-    static_pairs(1, COLS_AT, STATIC_COLS, range(NZ, NZ + nx))
+    static_pairs(1, COLS_AT, STATIC_COLS, range(NZ, NZ + 2 * nx))
     for copy in outgoing[NZ - 1 :]:
         copy.start()
     landed[z] = parts_ref[z]
-    landed[NZ + x] = parts_ref[NZ + x]
+    landed[NZ + mine] = parts_ref[NZ + mine]
     for copy in incoming:
         copy.wait_recv()
     total = landed[0]
-    for u in range(1, NZ + nx):
+    for u in range(1, NZ + 2 * nx):
         total = total + landed[u]
     for c in range(3):
         out_ref[c] = total[c * per_device : (c + 1) * per_device]
@@ -641,12 +612,12 @@
     counts_cols,
 ):
     _, per_device, size_block, conditions = source_strength.shape
-    units = SOURCES_Y + ny + nx
-    metas = NZ + nx + ny + 4
+    units = SOURCES_Y + ny + 2 * nx
+    metas = NZ + 2 * nx + ny + 2
     dma = pltpu.SemaphoreType.DMA
     any_space = pl.BlockSpec(memory_space=pl.ANY)
     hbm = pl.BlockSpec(memory_space=pltpu.HBM)
-    fars = (ny + 4) * per_device
+    fars = (ny + 2) * per_device
     small = pltpu.CompilerParams(vmem_limit_bytes=8 * 1024 * 1024)
     vmem = pl.BlockSpec(memory_space=pltpu.VMEM)
     blocks, own_axes, far_axes, listing = pl.pallas_call(
@@ -654,7 +625,7 @@
         name="gather",
         out_shape=(
             jax.ShapeDtypeStruct((units, per_device, size_block, conditions), jnp.bfloat16),
-            jax.ShapeDtypeStruct(((NZ + nx) * per_device, 8, 128), F32),
+            jax.ShapeDtypeStruct(((NZ + 2 * nx) * per_device, 8, 128), F32),
             jax.ShapeDtypeStruct((fars, size_block, 3 * 128), F32),
             jax.ShapeDtypeStruct((8, 128), jnp.int32),
         ),
@@ -668,16 +639,14 @@
             pltpu.VMEM((1, per_device), jnp.int32),
             pltpu.VMEM((2, 4 * per_device, 128), jnp.bfloat16),
             pltpu.VMEM((metas, 4 * per_device, 128), jnp.bfloat16),
-            dma((2, HALF + 1, per_device * SPLIT)),
+            dma((2, HALF + 1)),
             dma((2, HALF, per_device * SPLIT)),
+            dma((2, HALF)),
             dma((2, HALF, per_device * SPLIT)),
-            dma((2, HALF, per_device * SPLIT)),
-            dma((per_device * SPLIT + 1,)),
-            dma((per_device * SPLIT + 1,)),
             dma((max(ny - 1, 1),)),
             dma((max(ny - 1, 1),)),
-            dma((max(nx - 1, 1),)),
-            dma((max(nx - 1, 1),)),
+            dma((2 * nx - 1,)),
+            dma((2 * nx - 1,)),
             dma((metas,)),
             dma((metas,)),
             dma((3,)),
@@ -701,11 +670,11 @@
         )
     )
     rows = NZ * per_device
-    own = rows + nx * per_device
+    own = rows + 2 * nx * per_device
     shift = (SOURCES_Y + ny) * per_device - rows
     blocks = blocks.reshape(units * per_device, size_block, conditions)
     smem = pl.BlockSpec(memory_space=pltpu.SMEM)
-    parts_shape = (NZ + nx, 4 * per_device, 128)
+    parts_shape = (NZ + 2 * nx, 4 * per_device, 128)
     rest = pl.pallas_call(
         functools.partial(pair_kernel, rows, own, shift),
         name="pairs",
@@ -725,8 +694,8 @@
             pltpu.VMEM((128, 3 * 128), F32),
             pltpu.VMEM(parts_shape, F32),
             pltpu.VMEM(parts_shape, F32),
-            dma((NZ + nx,)),
-            dma((NZ + nx,)),
+            dma((NZ + 2 * nx,)),
+            dma((NZ + 2 * nx,)),
         ],
         compiler_params=pltpu.CompilerParams(
             collective_id=1, has_side_effects=True, vmem_limit_bytes=8 * 1024 * 1024

time: 75.3 us -> 73.9 us (0.981)
  Pallas kernels: 74.6 us -> 72.8 us
    pallas_call x1, Pallas kernels: 61.3 us -> 57.8 us  [shards(): pl.pallas_call(functools.partial(gather_kernel, nx, ny), name='gather', o...]
    pallas_call x1, Pallas kernels: 12.6 us -> 14.4 us  [shards(): pl.pallas_call(functools.partial(sums_kernel, nx, ny, rows, own, shift),...]
where the time goes in v5:
time: 73.9 us; the launch traced here: 73.5 us
  Pallas kernels  72.8 us (99%)
    pallas_call x1, Pallas kernels, shards(): pl.pallas_call(functools.partial(gather_kernel, nx, ny), name='gather', o...  57.8 us
    pallas_call x1, Pallas kernels, shards(): pl.pallas_call(functools.partial(sums_kernel, nx, ny, rows, own, shift),...  14.4 us

profile of v5, /device:TPU:1, one launch (start us, length us, event | category | flops | bytes accessed | tf_op | source)
XLA Modules:
  0.0 73.5 jit_solution(12947646375036455599)
XLA Ops:
  0.0 57.8 %gather.1 = (bf16[24,4,128,256]{3,2,1,0:T(8,128)(2,1)S(1)}, f32[64,8,128]{2,1,0:T(8,128)S(1)}, f32[24,128,384]{2,1,0:T(8,128)S(1)}, s32[8,128]{1,0:T(8,128)S(1)}) custom-call(bf16[4,128,256]{2,1,0:T(8,128)(2,1)} %bitcast.14, bf16[4,128,256]{2,1,0:T(8,128)(2,1)} %bitcast.15, bf16[3,4,128]{2,1,0:T(4,128)(2,1)} %bitcast.16, s32[4,32]{1,0:T(4,128)} %bitcast.17, ...), custom_call_target="tpu_custom_call" | custom-call | tf_op jit(solution)/shard_map/gather/pallas_call | solution.py:623
  57.8 0.6 pairs.1.rest_ref
  58.4 14.4 %sums.1 = f32[3,4,128]{2,1,0:T(4,128)S(1)} custom-call(s32[8,128]{1,0:T(8,128)S(1)} %get-tuple-element.9.list_ref.listing_ref, s32[8,128]{1,0:T(8,128)S(1)} %get-tuple-element.9.list_ref.listing_ref, bf16[96,128,256]{2,1,0:T(8,128)(2,1)S(1)} %bitcast.12, f32[64,8,128]{2,1,0:T(8,128)S(1)} %get-tuple-element.11.own_axes_ref, ...), custom_call_target="tpu_custom_call" | custom-call | tf_op jit(solution)/shard_map/sums/pallas_call | solution.py:687
  72.9 0.6 copy.9

commit v6 on v5

--- a/solution.py
+++ b/solution.py
@@ -189,8 +189,14 @@
     others_z, others_y, others_xc = place.others_z(), place.others_y(), place.others_xc()
     opposite = place.opposite()
     met = [device for _, device in others_z] + others_y + [device for _, _, device in others_xc]
-    met = met + [opposite, right, left]
+    met = met + [opposite]
+    crosses = (z == 0) | (z == NZ - 1)
+    over = place.at(z=NZ - 1 - z, h=1 - place.h)
     greet(met)
+
+    @pl.when(crosses)
+    def _():
+        greet([over])
 
     for copy in smalls:
         copy.wait()
@@ -200,7 +206,7 @@
     for which, mask in enumerate((row_mask, col_mask)):
         own_meta[which] = jnp.concatenate([points, mask], axis=0).astype(jnp.bfloat16)
 
-    await_greetings(len(met))
+    await_greetings(len(met) + crosses.astype(jnp.int32))
 
     def remote(src, dst, send, recv, device):
         return pltpu.make_async_remote_copy(

time: 73.9 us -> 73.5 us (level)
  no operation moved by 1% of the time
where the time goes in v6:
time: 73.5 us; the launch traced here: 73.3 us
  Pallas kernels  72.7 us (99%)
    pallas_call x1, Pallas kernels, shards(): pl.pallas_call(functools.partial(gather_kernel, nx, ny), name='gather', o...  57.8 us
    pallas_call x1, Pallas kernels, shards(): pl.pallas_call(functools.partial(sums_kernel, nx, ny, rows, own, shift),...  14.3 us

profile of v6, /device:TPU:1, one launch (start us, length us, event | category | flops | bytes accessed | tf_op | source)
XLA Modules:
  0.0 73.3 jit_solution(9439184263811236353)
XLA Ops:
  0.0 57.8 %gather.1 = (bf16[24,4,128,256]{3,2,1,0:T(8,128)(2,1)S(1)}, f32[64,8,128]{2,1,0:T(8,128)S(1)}, f32[24,128,384]{2,1,0:T(8,128)S(1)}, s32[8,128]{1,0:T(8,128)S(1)}) custom-call(bf16[4,128,256]{2,1,0:T(8,128)(2,1)} %bitcast.14, bf16[4,128,256]{2,1,0:T(8,128)(2,1)} %bitcast.15, bf16[3,4,128]{2,1,0:T(4,128)(2,1)} %bitcast.16, s32[4,32]{1,0:T(4,128)} %bitcast.17, ...), custom_call_target="tpu_custom_call" | custom-call | tf_op jit(solution)/shard_map/gather/pallas_call | solution.py:629
  57.8 0.6 pairs.1.rest_ref
  58.4 14.3 %sums.1 = f32[3,4,128]{2,1,0:T(4,128)S(1)} custom-call(s32[8,128]{1,0:T(8,128)S(1)} %get-tuple-element.9.list_ref.listing_ref, s32[8,128]{1,0:T(8,128)S(1)} %get-tuple-element.9.list_ref.listing_ref, bf16[96,128,256]{2,1,0:T(8,128)(2,1)S(1)} %bitcast.12, f32[64,8,128]{2,1,0:T(8,128)S(1)} %get-tuple-element.11.own_axes_ref, ...), custom_call_target="tpu_custom_call" | custom-call | tf_op jit(solution)/shard_map/sums/pallas_call | solution.py:693
  72.7 0.6 copy.9
